TPU v7x, 32 devices: a whole 2x2x4 slice. The times are simulated.
32 devices in a mesh: tm: 8 (over z, x), tmpl: 4 (over y, core).
Axes of the slice: x: 2, y: 2, z: 4, core: 2. Of those that a mesh axis runs over, the one named last changes fastest.
Arguments:
- records: float32 [4, 4608, 512], P('tmpl', 'tm'), may hold values from -6 to 6
- band_filter: float32 [65], replicated, may hold values from -0.75 to 0.75
- templates: bfloat16 [1024, 144, 128], P('tmpl'), may hold values from -6 to 6
- destinations: int32 [4, 4608], P('tmpl', 'tm'), may hold values from 0 to 7, as said below
- offsets: int32 [4, 4608], P('tmpl', 'tm'), may hold values from 0 to 294400, as said below
- live_counts: int32 [4, 8], P('tmpl', 'tm'), may hold values from 72 to 576, as said below
Outputs:
- detection: float32 [1024, 8192], P('tmpl', 'tm')
Inputs may be any that keep to these rules, and one draw needn't show every extreme that they name: `destinations`: device s's 576 entries of a quarter name every window exactly 72 times, so at most 72 live records go from one device to one window; in each quarter some window has all its entries live on every device. `offsets`: multiples of 512; within a quarter every pair of destination and offset occurs exactly once over all entries of all devices. The live entries of a device are its first live_counts entries; the others are absent records.
All inputs are finite; a program needn't handle non-finite values.
Results may differ from a plain program's by a relative error of at most 0.0029.
Values may be sent and summed in bfloat16 or wider, within the bound.
No kernel may reach another device: no remote copies, remote signals or barrier semaphores. Data moves between devices by JAX's collectives and lax.ppermute only.
A program may use at most 128 MiB of HBM per device.

v0:
```python
import jax
import jax.numpy as jnp
from jax import lax
from jax.sharding import PartitionSpec as P

CH = 144
DEC = 8
TAPS = 65


EPSILON = 1e-06


def passed_along(value, axis, steps):
    count = lax.axis_size(axis)
    initial, last = (max(0, -steps), min(count, count - steps))
    return lax.ppermute(value, axis, [(source, source + steps) for source in range(initial, last)])


def filter_phases(source, band_filter, count):
    rows = source.shape[0]
    blocks = (band_filter.shape[0] + DEC - 1) // DEC
    frames = count + blocks - 1
    needed = DEC * frames
    source = jnp.pad(source, ((0, 0), (0, needed - source.shape[1])))
    phased = source.reshape(rows, frames, DEC).transpose(0, 2, 1)
    taps_padded = jnp.pad(band_filter, (0, blocks * DEC - band_filter.shape[0])).reshape(
        blocks, DEC
    )
    result = jnp.zeros((rows, count), jnp.float32)
    for block in range(blocks):
        result = result + jnp.einsum(
            "rbn,b->rn",
            phased[:, :, block : block + count],
            taps_padded[block],
            precision=lax.Precision.HIGHEST,
        )
    return result


def arrange(arrived, arrived_labels, entries):
    flat = arrived.reshape(-1, arrived.shape[-1])
    names = arrived_labels.reshape(-1)
    target = jnp.where(names >= 0, names, entries).astype(jnp.int32)
    empty = jnp.zeros((entries + 1, flat.shape[1]), jnp.float32)
    return empty.at[target].set(flat)[:-1]


def shards(records, band_filter, templates, destinations, offsets, live_counts):
    stored = records[0]
    targets = destinations[0]
    starts = offsets[0]
    number = live_counts[0, 0]
    devices = lax.axis_size("tm")
    entries, rec_len = stored.shape
    capacity = entries // devices
    channels_here = CH // lax.axis_size("tmpl")
    slot_count = entries // channels_here
    window_len = slot_count * rec_len // DEC
    heads_len = (TAPS - 1) // DEC
    is_live = jnp.arange(entries, dtype=jnp.int32) < number
    member = (
        (targets[:, None] == jnp.arange(devices, dtype=jnp.int32)[None, :]) & is_live[:, None]
    ).astype(jnp.int32)
    order_in = jnp.sum(jnp.cumsum(member, 0) * member, 1) - 1
    placed = jnp.where(is_live, targets * capacity + order_in, devices * capacity)
    labels = (starts // rec_len).astype(jnp.float32)
    label_buf = (
        jnp.full((devices * capacity + 1,), -1.0, jnp.float32)
        .at[placed]
        .set(labels)[:-1]
        .reshape(devices, capacity)
    )
    padded = jnp.pad(stored, ((0, 0), (TAPS - 1, 0)))
    span = rec_len // DEC + heads_len
    partial_value = filter_phases(padded, band_filter, span)
    outgoing = (
        jnp.zeros((devices * capacity + 1, span), jnp.float32)
        .at[placed]
        .set(partial_value)[:-1]
        .reshape(devices, capacity, span)
    )
    arrived, arrived_labels = (
        lax.all_to_all(outgoing, "tm", split_axis=0, concat_axis=0, tiled=True),
        lax.all_to_all(label_buf, "tm", split_axis=0, concat_axis=0, tiled=True),
    )
    local = arrange(arrived, arrived_labels, entries).reshape(channels_here, slot_count, span)
    head_part = local[:, :, :heads_len]
    tail_part = local[:, :, heads_len:]
    following = passed_along(head_part[:, 0, :], "tm", -1)
    later = jnp.concatenate([head_part[:, 1:, :], following[:, None, :]], 1)
    tail_part = tail_part.at[:, :, rec_len // DEC - heads_len :].add(later)
    filtered = tail_part.reshape(channels_here, window_len)
    decim = filtered.astype(jnp.bfloat16)
    tlen = templates.shape[2]
    kept = templates.shape[0]
    width = min(16, tlen)
    after = passed_along(decim[:, : tlen - 1], "tm", -1)
    window_data = jnp.concatenate([decim, after], 1)
    piece = lax.all_gather(window_data, "tmpl", axis=0, tiled=True)
    corr = jnp.zeros((kept, window_len), jnp.float32)
    rows = piece.shape[0]

    def add_group(group, total):
        first = group * width
        block_tmpl = lax.dynamic_slice_in_dim(templates, first, width, 2).reshape(
            kept, rows * width
        )
        shifted = jnp.stack(
            [
                lax.dynamic_slice_in_dim(piece, first + shift_at, window_len, 1)
                for shift_at in range(width)
            ],
            1,
        )
        shifted = shifted.reshape(rows * width, window_len)
        return total + jnp.dot(block_tmpl, shifted, preferred_element_type=jnp.float32)

    corr = lax.fori_loop(0, tlen // width, add_group, corr)
    wide_piece = piece.astype(jnp.float32)
    corr, power = (corr, jnp.sum(wide_piece * wide_piece, 0))
    running = jnp.concatenate([jnp.zeros((1,), jnp.float32), jnp.cumsum(power)])
    energy = (running[tlen:] - running[:window_len]) / (CH * tlen)
    tscale = jnp.sqrt(jnp.mean(jnp.square(templates.astype(jnp.float32)), axis=(1, 2)) + EPSILON)
    return corr / (CH * tlen * tscale[:, None] * jnp.sqrt(energy + EPSILON)[None, :])


def solution(mesh):
    in_specs = (
        P("tmpl", "tm", None),
        P(),
        P("tmpl", None, None),
        P("tmpl", "tm"),
        P("tmpl", "tm"),
        P("tmpl", "tm"),
    )
    out_specs = P("tmpl", "tm")
    return jax.shard_map(shards, mesh=mesh, in_specs=in_specs, out_specs=out_specs, check_vma=False)
```

profile of v0, /device:TPU:0, one launch (start us, length us, event | category | flops | bytes accessed | tf_op | source)
XLA Modules:
  0.0 241.8 jit_solution(4960233261718359643)
XLA Ops:
  1.4 1.4 reduce-window.15
  4.8 4.1 %scatter_custom_fusion = f32[577]{0:T(1024)S(1)} fusion(s32[576]{0:T(1024)S(1)} %fusion.27, f32[576]{0:T(1024)S(1)} %fusion.21, f32[]{:T(128)} %constant.294.clone.1), kind=kCustom, calls=%fused_computation.85 | custom fusion | bytes 2312 | tf_op jit(solution)/shard_map/scatter | solution.py:71
  9.6 7.3 %all-to-all-start = ((f32[8,1,72]{2,1,0:T(1,128)}), f32[8,1,72]{2,1,0:T(1,128)S(1)}, u32[]{:S(2)}, u32[]{:S(2)}) async-start(f32[8,1,72]{2,1,0:T(1,128)} %all_to_all.9), calls=%async_computation | async-start | bytes 8192 | tf_op jit(solution)/shard_map/all_to_all | solution.py:85
  16.9 1.7 copy.34
  18.5 2.0 fusion.4
  20.6 2.0 fusion.5
  22.6 1.4 fusion.6
  24.0 1.4 fusion.7
  25.3 1.4 fusion.8
  26.7 1.4 fusion.9
  28.1 1.4 fusion.10
  29.4 1.3 fusion.11
  30.8 1.6 fusion.3
  33.9 4.5 %scatter_custom_fusion.1 = f32[577,72]{1,0:T(8,128)S(1)} fusion(s32[576]{0:T(1024)S(1)} %fusion.27, f32[1,576,72]{2,1,0:T(8,128)S(1)} %copy.46, f32[1,576,72]{2,1,0:T(8,128)S(1)} %copy.45, f32[1,576,72]{2,1,0:T(8,128)S(1)} %copy.44, f32[1,576,72]{2,1,0:T(8,128)S(1)} %copy.43, f32[1,576,72]{2,1,0:T(8,128)S(1)} %copy.42, f32[1,576,72]{2,1,0:T(8,128)S(1)} %copy.41, ...), kind=kCustom, calls=%fused_computation.38 | custom fusion | flops 331776 | bytes 2820388 | tf_op jit(solution)/shard_map/scatter | solution.py:80
  39.2 6.0 %all-to-all-start.1 = ((f32[8,72,72]{2,1,0:T(8,128)}), f32[8,72,72]{2,1,0:T(8,128)S(1)}, u32[]{:S(2)}, u32[]{:S(2)}) async-start(f32[8,72,72]{2,1,0:T(8,128)} %bitcast.28), calls=%async_computation.1 | async-start | bytes 589824 | tf_op jit(solution)/shard_map/all_to_all | solution.py:84
  46.6 7.6 %all-to-all-done.1 = f32[8,72,72]{2,1,0:T(8,128)S(1)} async-done(((f32[8,72,72]{2,1,0:T(8,128)}), f32[8,72,72]{2,1,0:T(8,128)S(1)}, u32[]{:S(2)}, u32[]{:S(2)}) %all-to-all-start.1) | async-done | bytes 165920 | tf_op jit(solution)/shard_map/all_to_all | solution.py:84
  54.2 4.2 %scatter_custom_fusion.2 = f32[577,72]{1,0:T(8,128)S(1)} fusion(s32[576]{0:T(1024)S(1)} %fusion.28, f32[576,72]{1,0:T(8,128)S(1)} %bitcast.198, f32[]{:T(128)} %constant.293.clone.1), kind=kCustom, calls=%fused_computation.47 | custom fusion | bytes 166180 | tf_op jit(solution)/shard_map/scatter | solution.py:46
  58.5 1.3 collective-permute-start
  59.8 5.9 %multiply_reduce_fusion = f32[256]{0:T(256)S(1)} fusion(bf16[256,144,128]{2,1,0:T(8,128)(2,1)} %param.12), kind=kLoop, calls=%fused_computation.23 | loop fusion | flops 14155520 | bytes 9438208 | tf_op jit(solution)/shard_map/reduce_sum | solution.py:124
  66.1 6.9 %scatter-add.4 = bf16[36,16,64]{2,1,0:T(8,128)(2,1)S(1)} dynamic-update-slice(bf16[36,16,64]{2,1,0:T(8,128)(2,1)S(1)} %slice.184, bf16[36,16,8]{2,1,0:T(8,128)(2,1)S(1)} %slice_add_fusion, s32[]{:T(128)} %constant.292.clone.1, s32[]{:T(128)} %constant.292.clone.1, s32[]{:T(128)} %constant.304.clone.1) | dynamic-update-slice | bytes 18436 | tf_op jit(solution)/shard_map/scatter-add | solution.py:92
  73.1 1.3 collective-permute-start.1
  74.4 13.9 %copy.37 = bf16[256,144,128]{0,1,2:T(8,128)(2,1)} copy(bf16[256,144,128]{2,1,0:T(8,128)(2,1)} %param.12) | data formatting | bytes 18874368
  88.4 6.4 %all-gather = bf16[4,36,1151]{2,1,0:T(8,128)(2,1)S(1)} all-gather(bf16[1,36,1151]{2,1,0:T(8,128)(2,1)S(1)} %maximum_bitcast_fusion), channel_id=1, replica_groups=mesh['tm'=8,'tmpl'=4] {'tmpl'}, dimensions={0}, use_global_device_ids=true | all-gather | bytes 414360 | tf_op jit(solution)/shard_map/all_gather | solution.py:100
  94.9 145.0 %while.17 = (s32[]{:T(128)}, f32[256,1024]{1,0:T(8,128)S(1)}, bf16[256,144,128]{0,1,2:T(8,128)(2,1)}, bf16[144,1151]{1,0:T(8,128)(2,1)S(1)}, s32[]{:T(128)}, /*i...) while((s32[]{:T(128)}, f32[256,1024]{1,0:T(8,128)S(1)}, ...), condition=%wide.region_7.8_spmd.clone, body=%wide.region_6.7_spmd.clone.sunk | while | flops 1208483968 | bytes 17433748 | solution.py:119
  99.5 0.9 bitcast_dynamic-update-slice_fusion.37
  104.7 0.9 bitcast_dynamic-update-slice_fusion.43
  109.1 4.2 %fusion.66 = f32[256,1024]{1,0:T(8,128)S(1)} fusion(bf16[144,16,1024]{2,0,1:T(8,128)(2,1)} %bitcast_dynamic-update-slice_fusion.47, bf16[256,144,128]{0,1,2:T(8,128)(2,1)} %get-tuple-element.288, s32[]{:T(128)S(6)} %select_n.290, f32[256,1024]{1,0:T(8,128)S(1)} %get-tuple-element.249, pred[]{:T(512)S(6)} %compare.15), kind=kOutput, calls=%fused_computation.4.clone.1 | convolution fusion | flops 1208483840 | bytes 7995397 | tf_op jit(solution)/shard_map/while/body/eval_jaxpr/dot_general | solution.py:117
  117.6 0.9 bitcast_dynamic-update-slice_fusion.37
  122.8 0.9 bitcast_dynamic-update-slice_fusion.43
  127.2 4.2 %fusion.66 = f32[256,1024]{1,0:T(8,128)S(1)} fusion(bf16[144,16,1024]{2,0,1:T(8,128)(2,1)} %bitcast_dynamic-update-slice_fusion.47, bf16[256,144,128]{0,1,2:T(8,128)(2,1)} %get-tuple-element.288, s32[]{:T(128)S(6)} %select_n.290, f32[256,1024]{1,0:T(8,128)S(1)} %get-tuple-element.249, pred[]{:T(512)S(6)} %compare.15), kind=kOutput, calls=%fused_computation.4.clone.1 | convolution fusion | flops 1208483840 | bytes 7995397 | tf_op jit(solution)/shard_map/while/body/eval_jaxpr/dot_general | solution.py:117
  135.7 0.9 bitcast_dynamic-update-slice_fusion.37
  140.9 0.9 bitcast_dynamic-update-slice_fusion.43
  145.3 4.2 %fusion.66 = f32[256,1024]{1,0:T(8,128)S(1)} fusion(bf16[144,16,1024]{2,0,1:T(8,128)(2,1)} %bitcast_dynamic-update-slice_fusion.47, bf16[256,144,128]{0,1,2:T(8,128)(2,1)} %get-tuple-element.288, s32[]{:T(128)S(6)} %select_n.290, f32[256,1024]{1,0:T(8,128)S(1)} %get-tuple-element.249, pred[]{:T(512)S(6)} %compare.15), kind=kOutput, calls=%fused_computation.4.clone.1 | convolution fusion | flops 1208483840 | bytes 7995397 | tf_op jit(solution)/shard_map/while/body/eval_jaxpr/dot_general | solution.py:117
  153.8 0.9 bitcast_dynamic-update-slice_fusion.37
  159.0 0.9 bitcast_dynamic-update-slice_fusion.43
  163.4 4.2 %fusion.66 = f32[256,1024]{1,0:T(8,128)S(1)} fusion(bf16[144,16,1024]{2,0,1:T(8,128)(2,1)} %bitcast_dynamic-update-slice_fusion.47, bf16[256,144,128]{0,1,2:T(8,128)(2,1)} %get-tuple-element.288, s32[]{:T(128)S(6)} %select_n.290, f32[256,1024]{1,0:T(8,128)S(1)} %get-tuple-element.249, pred[]{:T(512)S(6)} %compare.15), kind=kOutput, calls=%fused_computation.4.clone.1 | convolution fusion | flops 1208483840 | bytes 7995397 | tf_op jit(solution)/shard_map/while/body/eval_jaxpr/dot_general | solution.py:117
  171.9 0.9 bitcast_dynamic-update-slice_fusion.37
  177.1 0.9 bitcast_dynamic-update-slice_fusion.43
  181.4 4.2 %fusion.66 = f32[256,1024]{1,0:T(8,128)S(1)} fusion(bf16[144,16,1024]{2,0,1:T(8,128)(2,1)} %bitcast_dynamic-update-slice_fusion.47, bf16[256,144,128]{0,1,2:T(8,128)(2,1)} %get-tuple-element.288, s32[]{:T(128)S(6)} %select_n.290, f32[256,1024]{1,0:T(8,128)S(1)} %get-tuple-element.249, pred[]{:T(512)S(6)} %compare.15), kind=kOutput, calls=%fused_computation.4.clone.1 | convolution fusion | flops 1208483840 | bytes 7995397 | tf_op jit(solution)/shard_map/while/body/eval_jaxpr/dot_general | solution.py:117
  190.0 0.9 bitcast_dynamic-update-slice_fusion.37
  195.2 0.9 bitcast_dynamic-update-slice_fusion.43
  199.5 4.2 %fusion.66 = f32[256,1024]{1,0:T(8,128)S(1)} fusion(bf16[144,16,1024]{2,0,1:T(8,128)(2,1)} %bitcast_dynamic-update-slice_fusion.47, bf16[256,144,128]{0,1,2:T(8,128)(2,1)} %get-tuple-element.288, s32[]{:T(128)S(6)} %select_n.290, f32[256,1024]{1,0:T(8,128)S(1)} %get-tuple-element.249, pred[]{:T(512)S(6)} %compare.15), kind=kOutput, calls=%fused_computation.4.clone.1 | convolution fusion | flops 1208483840 | bytes 7995397 | tf_op jit(solution)/shard_map/while/body/eval_jaxpr/dot_general | solution.py:117
  208.1 0.9 bitcast_dynamic-update-slice_fusion.37
  213.3 0.9 bitcast_dynamic-update-slice_fusion.43
  217.6 4.2 %fusion.66 = f32[256,1024]{1,0:T(8,128)S(1)} fusion(bf16[144,16,1024]{2,0,1:T(8,128)(2,1)} %bitcast_dynamic-update-slice_fusion.47, bf16[256,144,128]{0,1,2:T(8,128)(2,1)} %get-tuple-element.288, s32[]{:T(128)S(6)} %select_n.290, f32[256,1024]{1,0:T(8,128)S(1)} %get-tuple-element.249, pred[]{:T(512)S(6)} %compare.15), kind=kOutput, calls=%fused_computation.4.clone.1 | convolution fusion | flops 1208483840 | bytes 7995397 | tf_op jit(solution)/shard_map/while/body/eval_jaxpr/dot_general | solution.py:117
  231.4 0.9 bitcast_dynamic-update-slice_fusion.43
  235.7 4.2 %fusion.66 = f32[256,1024]{1,0:T(8,128)S(1)} fusion(bf16[144,16,1024]{2,0,1:T(8,128)(2,1)} %bitcast_dynamic-update-slice_fusion.47, bf16[256,144,128]{0,1,2:T(8,128)(2,1)} %get-tuple-element.288, s32[]{:T(128)S(6)} %select_n.290, f32[256,1024]{1,0:T(8,128)S(1)} %get-tuple-element.249, pred[]{:T(512)S(6)} %compare.15), kind=kOutput, calls=%fused_computation.4.clone.1 | convolution fusion | flops 1208483840 | bytes 7995397 | tf_op jit(solution)/shard_map/while/body/eval_jaxpr/dot_general | solution.py:117
  240.6 1.2 multiply_divide_fusion
  (168 shorter events, 106.3 us)
Async XLA Ops:
  0.0 22.6 %copy-start = (f32[65]{0:T(128)S(1)}, f32[65]{0:T(128)}, u32[]{:S(2)}) copy-start(f32[65]{0:T(128)} %param.11) | copy-start | bytes 784
  9.6 29.6 %all-to-all-start = ((f32[8,1,72]{2,1,0:T(1,128)}), f32[8,1,72]{2,1,0:T(1,128)S(1)}, u32[]{:S(2)}, u32[]{:S(2)}) async-start(f32[8,1,72]{2,1,0:T(1,128)} %all_to_all.9), calls=%async_computation | async-start | bytes 8192 | tf_op jit(solution)/shard_map/all_to_all | solution.py:85
  39.2 15.0 %all-to-all-start.1 = ((f32[8,72,72]{2,1,0:T(8,128)}), f32[8,72,72]{2,1,0:T(8,128)S(1)}, u32[]{:S(2)}, u32[]{:S(2)}) async-start(f32[8,72,72]{2,1,0:T(8,128)} %bitcast.28), calls=%async_computation.1 | async-start | bytes 589824 | tf_op jit(solution)/shard_map/all_to_all | solution.py:84
  58.5 7.3 %collective-permute-start = (f32[36,8]{0,1:T(8,128)S(1)}, f32[36,8]{0,1:T(8,128)S(1)}, u32[]{:S(2)}, u32[]{:S(2)}) collective-permute-start(f32[36,8]{0,1:T(8,128)S(1)} %bitcast.203), channel_id=1, source_target_pairs={{4,0},{8,4},{12,8},{16,12},{20,16},{24,20},{28,24},{5,1},{9,5},{13... | collective-permute-start | bytes 3464 | tf_op jit(solution)/shard_map/ppermute | solution.py:17
  73.1 15.3 %collective-permute-start.1 = (bf16[36,127]{1,0:T(8,128)(2,1)S(1)}, bf16[36,127]{1,0:T(8,128)(2,1)S(1)}, u32[]{:S(2)}, u32[]{:S(2)}) collective-permute-start(bf16[36,127]{1,0:T(8,128)(2,1)S(1)} %slice.188), channel_id=1, source_target_pairs={{4,0},{8,4},{12,8},{16,12},{20,16},{24,20},{28,24},{5,1},{9,5},{13... | collective-permute-start | bytes 27440 | tf_op jit(solution)/shard_map/ppermute | solution.py:17
where the time goes:
time: 245 us; the launch traced here: 242 us
  local copies, waits for them, and re-layouts  146 us (60%)
  matrix products  47.1 us (19%)
  other arithmetic  16.8 us (7%)
  starting transfers between devices  15.8 us (6%)
  waiting for transfers between devices  7.61 us (3%)
  blocking collectives  6.35 us (3%)
    while x120, local copies, waits for them, and re-layouts  104 us
    dot_general x8, matrix products, add_group(): jnp.dot(block_tmpl, shifted, preferred_element_type=jnp.float32)  33.4 us
    unnamed x5, local copies, waits for them, and re-layouts  15.7 us
    dot_general x9, matrix products, filter_phases(): jnp.einsum('rbn,b->rn', phased[:, :, block:block + count], taps_padded[bl...  13.7 us
    all_to_all x1, waiting for transfers between devices, shards(): lax.all_to_all(outgoing, 'tm', split_axis=0, concat_axis=0, tiled=True)  7.6 us
    all_to_all x1, starting transfers between devices, shards(): lax.all_to_all(label_buf, 'tm', split_axis=0, concat_axis=0, tiled=True)  7.25 us
    scatter-add x1, local copies, waits for them, and re-layouts, shards(): tail_part = tail_part.at[:, :, rec_len // DEC - heads_len:].add(later)  6.88 us
    another operation x8, local copies, waits for them, and re-layouts, add_group(): jnp.stack([lax.dynamic_slice_in_dim(piece, first + shift_at, window_len,...  6.82 us
  transfers between devices with their start and end apart: 4, of which 1 were waited for; matrix products, arithmetic and copies ran while one was open for 18% of the time, Pallas kernels for 0%

commit v1 on v0

v1 whole, which is shorter than its diff:
```python
import functools

import jax
import jax.numpy as jnp
from jax import lax
from jax.experimental import pallas as pl
from jax.experimental.pallas import tpu as pltpu
from jax.sharding import PartitionSpec as P

CH = 144
DEC = 8
TAPS = 65
EPSILON = 1e-06

LANES = 128
CHUNK = 16
HEAD = (TAPS - 1) // DEC
GROUP = 12
MIB = 2**20
BF = jnp.bfloat16
F32 = jnp.float32


def whole(space=pltpu.VMEM):
    return pl.BlockSpec(memory_space=space)


def lane_of(shape):
    return lax.broadcasted_iota(jnp.int32, shape, len(shape) - 1)


def row_of(channel):
    row = channel
    for first in range(GROUP, CH, GROUP):
        row = row + jnp.where(channel >= first, CHUNK - GROUP, 0)
    return row


def flip(values):
    lane = lane_of(values.shape)
    return jnp.take_along_axis(values, lane + (CHUNK - 1) - 2 * (lane % CHUNK), 1)


def turn(rows):
    chunk = lane_of((1, LANES)) // CHUNK
    rows = list(rows)
    step = 1
    while step < len(rows):
        odd = (chunk // step) % 2 == 1
        shift = CHUNK * step
        for low in range(len(rows)):
            if low & step:
                continue
            first, second = rows[low], rows[low + step]
            rows[low] = jnp.where(odd, pltpu.roll(second, shift, 1), first)
            rows[low + step] = jnp.where(odd, second, pltpu.roll(first, LANES - shift, 1))
        step *= 2
    return rows


def pack_kernel(slots, windows, live_ref, record_ref, band_ref, window_ref, start_ref, out_ref, taps, labels):
    entries, rec_len = record_ref.shape[1:]
    span = rec_len // DEC
    capacity = entries // windows
    stride = 2 * capacity
    width = taps.shape[1]

    taps[...] = jnp.zeros_like(taps)
    taps[0:1, 0:TAPS] = band_ref[...].reshape(1, TAPS)
    base = jnp.broadcast_to(taps[0:1, :], taps.shape)
    firsts = list(range(HEAD, HEAD + span, 8)) + [0, span, 0, span, 0]
    bands = [
        pltpu.roll(base, (DEC * first - DEC * HEAD) % width, 1, stride=DEC, stride_axis=0)[:, :rec_len]
        for first in firsts
    ]
    bands.append(jnp.zeros((LANES - 8 * len(firsts), rec_len), F32))
    filters = jnp.concatenate(bands, 0)
    value = lax.dot_general(
        record_ref[0],
        filters,
        (((1,), (1,)), ((), ())),
        precision=lax.Precision.HIGHEST,
        preferred_element_type=F32,
    )
    high = value.astype(BF).astype(F32)
    rest = value - high
    middle = rest.astype(BF).astype(F32)
    low = rest - middle

    window = window_ref[...]
    label = start_ref[...] // rec_len
    channel = label // slots
    slot = label - channel * slots
    labels[...] = jnp.zeros_like(labels)
    mark = span + 5 * HEAD
    labels[mark : mark + 1, 0:entries] = (slot + 1).astype(F32)
    labels[mark + 1 : mark + 2, 0:entries] = row_of(channel).astype(F32)
    marks = labels[...].T[:entries]
    lane = lane_of(value.shape)
    payload = jnp.where(
        lane < span + HEAD,
        high,
        jnp.where(lane < span + 3 * HEAD, middle, jnp.where(lane < mark, low, marks)),
    ).astype(BF)

    live = lane_of((1, entries)) < live_ref[0, 0]
    each = lax.broadcasted_iota(jnp.int32, (windows, entries), 0)
    member = (window == each) & live
    ahead = (window == each + 1) & live & (slot < 3)
    both = jnp.concatenate([jnp.where(member, 1.0, 0.0), jnp.where(ahead, 1.0, 0.0)], 0)
    before = lax.broadcasted_iota(jnp.int32, (entries, entries), 0) <= lane_of((entries, entries))
    count = jnp.dot(both.astype(BF), jnp.where(before, 1.0, 0.0).astype(BF), preferred_element_type=F32)
    first = (each * stride).astype(F32)
    place = jnp.sum(jnp.where(member, count[:windows] + first, 0.0), 0, keepdims=True) - 1.0
    place_ahead = (
        jnp.sum(jnp.where(ahead, count[windows:] + (first + capacity), 0.0), 0, keepdims=True) - 1.0
    )
    total = out_ref.shape[0]
    part = total // 4
    for index in range(4):
        row = (lax.broadcasted_iota(jnp.int32, (part, entries), 0) + index * part).astype(F32)
        chosen = jnp.where((row == place) | (row == place_ahead), 1.0, 0.0).astype(BF)
        out_ref[index * part : (index + 1) * part, :] = jnp.dot(
            chosen, payload, preferred_element_type=F32
        ).astype(BF)


def pack(records, band_filter, windows_of, starts, live, slots, windows):
    entries, rec_len = records.shape[1:]
    return pl.pallas_call(
        functools.partial(pack_kernel, slots, windows),
        out_shape=jax.ShapeDtypeStruct((2 * entries, LANES), BF),
        in_specs=[whole(pltpu.SMEM), whole(), whole(), whole(), whole()],
        out_specs=whole(),
        scratch_shapes=[
            pltpu.VMEM((8, rec_len + LANES), F32),
            pltpu.VMEM((LANES, pl.cdiv(entries, LANES) * LANES), F32),
        ],
        compiler_params=pltpu.CompilerParams(vmem_limit_bytes=24 * MIB),
    )(live, records, band_filter, windows_of, starts)


def arrange_kernel(slots, stride, arrived_ref, out_ref):
    total = arrived_ref.shape[0]
    rows = out_ref.shape[1]
    blocks = out_ref.shape[0] - 1
    span = LANES // 2
    mark = span + 5 * HEAD
    arrived = arrived_ref[...]
    lane = lane_of((8, LANES))
    weigh = jnp.where(lane == mark, float(rows), jnp.where(lane == mark + 1, 1.0, 0.0)).astype(BF)
    name = lax.dot_general(weigh, arrived, (((1,), (1,)), ((), ())), preferred_element_type=F32)[0:1]
    ahead = lane_of((1, total)) % stride >= stride // 2
    target = jnp.where(name > 0, name - rows + jnp.where(ahead, float(slots * rows), 0.0), -1.0)
    held = slots + 3
    row = lax.broadcasted_iota(jnp.int32, (held * rows, total), 0).astype(F32)
    chosen = jnp.where(row == target, 1.0, 0.0).astype(BF)
    placed = jnp.dot(chosen, arrived, preferred_element_type=F32)
    lane = lane_of((rows, LANES))
    own = []
    previous = None
    for slot in range(held):
        part = placed[slot * rows : (slot + 1) * rows]
        summed = (
            part
            + pltpu.roll(part, LANES - 2 * HEAD, 1)
            + pltpu.roll(part, LANES - 4 * HEAD, 1)
        )
        if previous is not None:
            kept, tail = previous
            tail = tail + pltpu.roll(summed, LANES - HEAD, 1)
            own.append(jnp.where(lane < span - HEAD, kept, tail))
        previous = part, summed
    pairs = []
    for index in range(0, slots + 2, 2):
        pairs.append(jnp.where(lane < span, own[index], pltpu.roll(own[index + 1], span, 1)))
    turned = turn(pairs[:blocks])
    for index, value in enumerate(turned + pairs[blocks:]):
        out_ref[index] = flip(value).astype(BF)


def arrange(arrived, slots, stride, rows):
    total = arrived.shape[0]
    return pl.pallas_call(
        functools.partial(arrange_kernel, slots, stride),
        out_shape=jax.ShapeDtypeStruct((slots // 2 + 1, rows, LANES), BF),
        in_specs=[whole()],
        out_specs=whole(),
        compiler_params=pltpu.CompilerParams(vmem_limit_bytes=32 * MIB),
    )(arrived)


def regroup_kernel(template_ref, out_ref, square_ref, wide):
    kept, channels, tlen = template_ref.shape
    wide[...] = template_ref[...].astype(F32).reshape(kept * channels, tlen)
    total = jnp.zeros((kept, tlen), F32)
    for channel in range(channels):
        taps = wide[pl.ds(channel, kept, stride=channels), :]
        total = total + taps * taps
        side = (channel % 2) * tlen
        out_ref[channel // 2, :, side : side + tlen] = taps.astype(BF)
    step = pl.program_id(0)

    @pl.when(step == 0)
    def _():
        square_ref[...] = total

    @pl.when(step > 0)
    def _():
        square_ref[...] += total


def regroup(templates):
    kept, channels, tlen = templates.shape
    return pl.pallas_call(
        regroup_kernel,
        grid=(channels // CHUNK,),
        in_specs=[pl.BlockSpec((kept, CHUNK, tlen), lambda i: (0, i, 0))],
        out_specs=[
            pl.BlockSpec((CHUNK // 2, kept, 2 * tlen), lambda i: (i, 0, 0)),
            pl.BlockSpec((kept, tlen), lambda i: (0, 0)),
        ],
        out_shape=[
            jax.ShapeDtypeStruct((channels // 2, kept, 2 * tlen), BF),
            jax.ShapeDtypeStruct((kept, tlen), F32),
        ],
        scratch_shapes=[pltpu.VMEM((kept * CHUNK, tlen), F32)],
        compiler_params=pltpu.CompilerParams(vmem_limit_bytes=24 * MIB),
    )(templates)


def shifted(here, there, row, out):
    step = lax.broadcasted_iota(jnp.int32, (8, LANES), 0)
    within = lane_of((8, LANES)) % CHUNK
    blocks = out.shape[1] // CHUNK
    for side in range(2):
        for block in range(blocks):
            one = jnp.broadcast_to(here[block, pl.ds(row + side, 1), :], (8, LANES))
            other = jnp.broadcast_to(there[block + 1, pl.ds(row + side, 1), :], (8, LANES))
            halves = [
                pltpu.roll(jnp.where(within < CHUNK - first - step, one, other), first, 1, stride=1, stride_axis=0)
                for first in (0, 8)
            ]
            out[side, CHUNK * block : CHUNK * (block + 1), :] = jnp.concatenate(halves, 0).astype(BF)


def correlate_kernel(
    sample_ref, square_ref, template_ref, out_ref, held, here, there, even, odd, scale, arrivals
):
    quarters, blocks, rows = sample_ref.shape[:3]
    blocks -= 1
    groups = arrivals.shape[0]
    pairs = GROUP // 2
    tlen = square_ref.shape[1]

    def fetch(group):
        part = pl.ds(group * pairs, pairs)
        return pltpu.make_async_copy(template_ref.at[part], held.at[part], arrivals.at[group])

    for group in range(groups):
        fetch(group).start()
    lane = lane_of((1, LANES))
    after_power = jnp.zeros((1, LANES), F32)
    for quarter in range(quarters):
        part = slice(rows * quarter, rows * (quarter + 1))
        after = sample_ref[quarter, blocks].astype(F32)
        after_power = after_power + jnp.sum(after * after, 0, keepdims=True)
        for block in range(blocks):
            value = sample_ref[quarter, block].astype(F32)
            following = jnp.where(
                lane >= LANES - CHUNK,
                pltpu.roll(after, (LANES - CHUNK - CHUNK * block) % LANES, 1),
                pltpu.roll(value, LANES - CHUNK, 1),
            )
            here[block, part] = value
            here[block + blocks, part] = following
            there[block, part] = pltpu.roll(value, LANES - CHUNK, 1)
            there[block + blocks, part] = pltpu.roll(following, LANES - CHUNK, 1)
    power = [jnp.sum(here[block] * here[block], 0, keepdims=True) for block in range(blocks)]
    power = [flip(jnp.broadcast_to(line, (8, LANES)))[0:1] for line in turn(power) + [after_power]]
    later = jnp.concatenate(power[:blocks], 0)
    earlier = jnp.concatenate(power[1:], 0)
    step = 1
    while step < LANES:
        later = later + jnp.where(lane < LANES - step, pltpu.roll(later, LANES - step, 1), 0.0)
        earlier = earlier + jnp.where(lane >= step, pltpu.roll(earlier, step, 1), 0.0)
        step *= 2
    earlier = jnp.where(lane >= 1, pltpu.roll(earlier, 1, 1), 0.0)
    norm = float(CH * tlen)
    scale[...] = lax.rsqrt((later + earlier) / norm + EPSILON) / norm

    def products(*sums):
        shifted(here, there, 0, even)

        def one_group(group, carry):
            fetch(group).wait()
            for pair in range(pairs):
                now, then = (even, odd) if pair % 2 == 0 else (odd, even)
                taps = held[group * pairs + pair]
                for stage in range(2):
                    for unit in range(2):
                        first = 2 * (2 * unit + stage)
                        columns = [
                            jnp.concatenate(
                                [now[side, CHUNK * block : CHUNK * block + tlen, :] for side in range(2)], 0
                            )
                            for block in (first, first + 1)
                        ]
                        pltpu.matmul_push_rhs(jnp.concatenate(columns, 1), stage, unit)
                    for unit in range(2):
                        pltpu.matmul_acc_lhs(sums[2 * unit + stage], taps, load_staged_rhs=stage)
                if pair < pairs - 1:
                    row = group * CHUNK + 2 * (pair + 1)
                else:
                    row = jnp.minimum(group + 1, groups - 1) * CHUNK
                shifted(here, there, row, then)
            return carry

        lax.fori_loop(0, groups, one_group, 0)
        results = []
        for total in sums:
            value = pltpu.matmul_pop(total)
            results += [value[:, :LANES], value[:, LANES:]]
        template_scale = lax.rsqrt(jnp.sum(square_ref[...], 1, keepdims=True) / norm + EPSILON)
        for block, value in enumerate(turn(results)):
            out_ref[:, LANES * block : LANES * (block + 1)] = (
                flip(value) * template_scale * scale[block : block + 1, :]
            )

    kept = out_ref.shape[0]
    pl.run_scoped(
        products, *[pltpu.ACC(unit)((kept, 2 * LANES), F32) for unit in (0, 0, 1, 1)]
    )


def correlate(samples, squares, templates):
    pairs, kept, width = templates.shape
    quarters, blocks, rows = samples.shape[:3]
    blocks -= 1
    tlen = width // 2
    here = pltpu.VMEM((2 * blocks, quarters * rows, LANES), F32)
    shifts = pltpu.VMEM((2, CHUNK * (2 * blocks - 1), LANES), BF)
    return pl.pallas_call(
        correlate_kernel,
        out_shape=jax.ShapeDtypeStruct((kept, blocks * LANES), F32),
        in_specs=[whole(), whole(), whole(pl.ANY)],
        out_specs=whole(),
        scratch_shapes=[
            pltpu.VMEM(templates.shape, BF),
            here,
            here,
            shifts,
            shifts,
            pltpu.VMEM((blocks, LANES), F32),
            pltpu.SemaphoreType.DMA((2 * pairs // GROUP,)),
        ],
        compiler_params=pltpu.CompilerParams(vmem_limit_bytes=48 * MIB),
    )(samples, squares, templates)


def shards(records, band_filter, templates, destinations, offsets, live_counts):
    windows = lax.axis_size("tm")
    quarters = lax.axis_size("tmpl")
    entries, rec_len = records.shape[1:]
    channels = CH // quarters
    slots = entries // channels
    stride = 2 * (entries // windows)
    rows = channels // GROUP * CHUNK
    outgoing = pack(records, band_filter, destinations, offsets, live_counts, slots, windows)
    outgoing = outgoing.reshape(windows, stride, LANES)
    arrived = lax.all_to_all(outgoing, "tm", split_axis=0, concat_axis=0, tiled=True)
    grouped, squares = regroup(templates)
    samples = arrange(arrived.reshape(2 * entries, LANES), slots, stride, rows)
    samples = lax.all_gather(samples, "tmpl", axis=0, tiled=False)
    return correlate(samples, squares, grouped)


def solution(mesh):
    in_specs = (
        P("tmpl", "tm", None),
        P(),
        P("tmpl", None, None),
        P("tmpl", "tm"),
        P("tmpl", "tm"),
        P("tmpl", "tm"),
    )
    out_specs = P("tmpl", "tm")
    inner = jax.shard_map(shards, mesh=mesh, in_specs=in_specs, out_specs=out_specs, check_vma=False)
    return inner
```

time: 245 us -> 57.3 us (0.23); the launches traced: 242 us -> 56.9 us
  local copies, waits for them, and re-layouts: 146 us -> 10.6 us
  matrix products: 47.1 us -> 0 us
  Pallas kernels: 0 us -> 31.6 us
  other arithmetic: 16.8 us -> 0 us
  starting transfers between devices: 15.8 us -> 7.25 us
  waiting for transfers between devices: 7.61 us -> 0.01 us
    while x120 -> x0, local copies, waits for them, and re-layouts: 104 us -> none
    dot_general x17 -> x0, matrix products: 47.1 us -> none  [the longest x8 33.4 us: add_group(): jnp.dot(block_tmpl, shifted, preferred_element_type=jnp.float32)]
    pallas_call x0 -> x4, Pallas kernels: none -> 31.6 us  [the longest x1 15.8 us: correlate(): pl.pallas_call(correlate_kernel, out_shape=jax.ShapeDtypeStruct((kept, bl...]
    scatter x2 -> x0, local copies, waits for them, and re-layouts: 8.3 us -> none  [the longest x1 4.2 us: arrange(): return empty.at[target].set(flat)[:-1]]
    all_to_all x1, waiting for transfers between devices: 7.6 us -> 0.01 us  [shards(): lax.all_to_all(outgoing, 'tm', split_axis=0, concat_axis=0, tiled=True)]
    another operation x14 -> x0, local copies, waits for them, and re-layouts: 7.31 us -> none  [the longest x8 6.82 us: add_group(): jnp.stack([lax.dynamic_slice_in_dim(piece, first + shift_at, window_len,...]
    all_to_all x1 -> x0, starting transfers between devices: 7.25 us -> none  [shards(): lax.all_to_all(label_buf, 'tm', split_axis=0, concat_axis=0, tiled=True)]
    scatter-add x1 -> x0, local copies, waits for them, and re-layouts: 6.88 us -> none  [shards(): tail_part = tail_part.at[:, :, rec_len // DEC - heads_len:].add(later)]
  transfers between devices with their start and end apart: 4 -> 1, of which waited for: 1 -> 0; matrix products, arithmetic and copies ran while one was open for 18% -> 0% of each run, Pallas kernels for 0% -> 19%
where the time goes in v1:
time: 57.3 us; the launch traced here: 56.9 us
  Pallas kernels  31.6 us (55%)
  local copies, waits for them, and re-layouts  10.6 us (18%)
  starting transfers between devices  7.25 us (13%)
  blocking collectives  6.76 us (12%)
  between operations  0.69 us (1%)
    pallas_call x1, Pallas kernels, correlate(): pl.pallas_call(correlate_kernel, out_shape=jax.ShapeDtypeStruct((kept, bl...  15.8 us
    pallas_call x1, Pallas kernels, regroup(): pl.pallas_call(regroup_kernel, grid=(channels // CHUNK,), in_specs=[pl.Bl...  11 us
    unnamed x12, local copies, waits for them, and re-layouts  10.6 us
    all_to_all x1, starting transfers between devices, shards(): lax.all_to_all(outgoing, 'tm', split_axis=0, concat_axis=0, tiled=True)  7.25 us
    all_gather x1, blocking collectives, shards(): samples = lax.all_gather(samples, 'tmpl', axis=0, tiled=False)  6.76 us
    pallas_call x1, Pallas kernels, pack(): pl.pallas_call(functools.partial(pack_kernel, slots, windows), out_shape=...  3.26 us
    pallas_call x1, Pallas kernels, arrange(): pl.pallas_call(functools.partial(arrange_kernel, slots, stride), out_shap...  1.58 us
  transfers between devices with their start and end apart: 1, of which 0 were waited for; matrix products, arithmetic and copies ran while one was open for 0% of the time, Pallas kernels for 19%

profile of v1, /device:TPU:0, one launch (start us, length us, event | category | flops | bytes accessed | tf_op | source)
XLA Modules:
  0.0 56.9 jit_solution(3486866372720208999)
XLA Ops:
  0.7 0.0 copy-start.2
  0.7 1.3 %copy-done.2 = f32[1,576,512]{2,1,0:T(8,128)S(1)} copy-done((f32[1,576,512]{2,1,0:T(8,128)S(1)}, f32[1,576,512]{2,1,0:T(8,128)}, u32[]{:S(2)}) %copy-start.2) | copy-done | bytes 1179672
  1.9 0.0 copy-start.3
  1.9 0.7 %copy-done.3 = s32[1,576]{1,0:T(1,128)S(1)} copy-done((s32[1,576]{1,0:T(1,128)S(1)}, s32[1,576]{1,0:T(1,128)}, u32[]{:S(2)}) %copy-start.3) | copy-done | bytes 2328
  2.6 0.0 copy-start.4
  2.6 0.7 %copy-done.4 = s32[1,576]{1,0:T(1,128)S(1)} copy-done((s32[1,576]{1,0:T(1,128)S(1)}, s32[1,576]{1,0:T(1,128)}, u32[]{:S(2)}) %copy-start.4) | copy-done | bytes 2328
  3.3 0.0 copy-start.5
  3.3 0.7 %copy-done.5 = f32[65]{0:T(128)S(1)} copy-done((f32[65]{0:T(128)S(1)}, f32[65]{0:T(128)}, u32[]{:S(2)}) %copy-start.5) | copy-done | bytes 284
  3.9 3.3 %shard_map.64 = bf16[1152,128]{1,0:T(8,128)(2,1)} custom-call(s32[1,1]{1,0:T(1,128)S(6)} %copy.7.live_ref, f32[1,576,512]{2,1,0:T(8,128)S(1)} %copy-done.2, f32[65]{0:T(128)S(1)} %copy-done.5, s32[1,576]{1,0:T(1,128)S(1)} %copy-done.3, s32[1,576]{1,0:T(1,128)S(1)} %copy-done.4), custom_call_target="tpu_custom_call" | custom-call | tf_op jit(solution)/shard_map/pallas_call | solution.py:130
  7.2 7.3 %all-to-all-start = ((bf16[8,144,128]{2,1,0:T(8,128)(2,1)}), bf16[8,144,128]{2,1,0:T(8,128)(2,1)S(1)}, u32[]{:S(2)}, u32[]{:S(2)}) async-start(bf16[8,144,128]{2,1,0:T(8,128)(2,1)} %bitcast), calls=%async_computation | async-start | bytes 589824 | tf_op jit(solution)/shard_map/all_to_all | solution.py:371
  14.5 0.0 copy-start
  14.5 3.7 %copy-done = bf16[256,144,128]{2,1,0:T(8,128)(2,1)S(1)} copy-done((bf16[256,144,128]{2,1,0:T(8,128)(2,1)S(1)}, bf16[256,144,128]{2,1,0:T(8,128)(2,1)}, u32[]{:S(2)}) %copy-start) | copy-done | bytes 9437208
  18.1 11.0 %shard_map.66 = (bf16[72,256,256]{2,1,0:T(8,128)(2,1)S(1)}, f32[256,128]{1,0:T(8,128)S(1)}) custom-call(bf16[256,144,128]{2,1,0:T(8,128)(2,1)S(1)} %copy-done), custom_call_target="tpu_custom_call" | custom-call | tf_op jit(solution)/shard_map/pallas_call | solution.py:215
  29.1 0.0 copy-start.1
  29.1 3.6 %copy-done.1 = bf16[72,256,256]{2,1,0:T(8,128)(2,1)} copy-done((bf16[72,256,256]{2,1,0:T(8,128)(2,1)}, bf16[72,256,256]{2,1,0:T(8,128)(2,1)S(1)}, u32[]{:S(2)}) %copy-start.1) | copy-done | bytes 9437208
  32.8 0.0 all-to-all-done
  32.8 1.6 %shard_map.65 = bf16[9,48,128]{2,1,0:T(8,128)(2,1)S(1)} custom-call(bf16[1152,128]{1,0:T(8,128)(2,1)S(1)} %bitcast.4), custom_call_target="tpu_custom_call" | custom-call | tf_op jit(solution)/shard_map/pallas_call | solution.py:184
  34.4 6.8 %all-gather = bf16[36,48,128]{2,1,0:T(8,128)(2,1)S(1)} all-gather(bf16[9,48,128]{2,1,0:T(8,128)(2,1)S(1)} %shard_map.65), channel_id=2, replica_groups=mesh['tm'=8,'tmpl'=4] {'tmpl'}, dimensions={0}, use_global_device_ids=true | all-gather | bytes 552960 | tf_op jit(solution)/shard_map/all_gather | solution.py:374
  41.1 15.8 %shard_map.67 = f32[256,1024]{1,0:T(8,128)} custom-call(bf16[4,9,48,128]{3,2,1,0:T(8,128)(2,1)S(1)} %bitcast.3, f32[256,128]{1,0:T(8,128)S(1)} %get-tuple-element.7.square_ref, bf16[72,256,256]{2,1,0:T(8,128)(2,1)} %copy-done.1), custom_call_target="tpu_custom_call" | custom-call | tf_op jit(solution)/shard_map/pallas_call | solution.py:343
Async XLA Ops:
  0.7 1.3 %copy-start.2 = (f32[1,576,512]{2,1,0:T(8,128)S(1)}, f32[1,576,512]{2,1,0:T(8,128)}, u32[]{:S(2)}) copy-start(f32[1,576,512]{2,1,0:T(8,128)} %record_ref.1) | copy-start | bytes 3538948
  1.9 0.7 %copy-start.3 = (s32[1,576]{1,0:T(1,128)S(1)}, s32[1,576]{1,0:T(1,128)}, u32[]{:S(2)}) copy-start(s32[1,576]{1,0:T(1,128)} %window_ref.1) | copy-start | bytes 6916
  2.6 0.7 %copy-start.4 = (s32[1,576]{1,0:T(1,128)S(1)}, s32[1,576]{1,0:T(1,128)}, u32[]{:S(2)}) copy-start(s32[1,576]{1,0:T(1,128)} %start_ref.1) | copy-start | bytes 6916
  3.3 0.7 %copy-start.5 = (f32[65]{0:T(128)S(1)}, f32[65]{0:T(128)}, u32[]{:S(2)}) copy-start(f32[65]{0:T(128)} %band_ref.1) | copy-start | bytes 784
  7.2 25.6 %all-to-all-start = ((bf16[8,144,128]{2,1,0:T(8,128)(2,1)}), bf16[8,144,128]{2,1,0:T(8,128)(2,1)S(1)}, u32[]{:S(2)}, u32[]{:S(2)}) async-start(bf16[8,144,128]{2,1,0:T(8,128)(2,1)} %bitcast), calls=%async_computation | async-start | bytes 589824 | tf_op jit(solution)/shard_map/all_to_all | solution.py:371
  14.5 3.7 %copy-start = (bf16[256,144,128]{2,1,0:T(8,128)(2,1)S(1)}, bf16[256,144,128]{2,1,0:T(8,128)(2,1)}, u32[]{:S(2)}) copy-start(bf16[256,144,128]{2,1,0:T(8,128)(2,1)} %template_ref.1) | copy-start | bytes 28311556
  29.1 3.6 %copy-start.1 = (bf16[72,256,256]{2,1,0:T(8,128)(2,1)}, bf16[72,256,256]{2,1,0:T(8,128)(2,1)S(1)}, u32[]{:S(2)}) copy-start(bf16[72,256,256]{2,1,0:T(8,128)(2,1)S(1)} %get-tuple-element.8.template_ref) | copy-start | bytes 28311556

commit v2 on v1

v2 whole, which is shorter than its diff:
```python
import functools

import jax
import jax.numpy as jnp
from jax import lax
from jax.experimental import pallas as pl
from jax.experimental.pallas import tpu as pltpu
from jax.sharding import PartitionSpec as P

CH = 144
DEC = 8
TAPS = 65
EPSILON = 1e-06

LANES = 128
CHUNK = 16
HEAD = (TAPS - 1) // DEC
GROUP = 12
MIB = 2**20
BF = jnp.bfloat16
F32 = jnp.float32


def whole(space=pltpu.VMEM):
    return pl.BlockSpec(memory_space=space)


def lane_of(shape):
    return lax.broadcasted_iota(jnp.int32, shape, len(shape) - 1)


def row_of(channel):
    row = channel
    for first in range(GROUP, CH, GROUP):
        row = row + jnp.where(channel >= first, CHUNK - GROUP, 0)
    return row


def flip(values):
    lane = lane_of(values.shape)
    return jnp.take_along_axis(values, lane + (CHUNK - 1) - 2 * (lane % CHUNK), 1)


def turn(rows):
    chunk = lane_of((1, LANES)) // CHUNK
    rows = list(rows)
    step = 1
    while step < len(rows):
        odd = (chunk // step) % 2 == 1
        shift = CHUNK * step
        for low in range(len(rows)):
            if low & step:
                continue
            first, second = rows[low], rows[low + step]
            rows[low] = jnp.where(odd, pltpu.roll(second, shift, 1), first)
            rows[low + step] = jnp.where(odd, second, pltpu.roll(first, LANES - shift, 1))
        step *= 2
    return rows


def pack_kernel(
    slots,
    windows,
    live_hbm,
    record_hbm,
    band_hbm,
    window_hbm,
    start_hbm,
    out_ref,
    live_ref,
    record_ref,
    band_ref,
    window_ref,
    start_ref,
    taps,
    labels,
    arrivals,
):
    entries, rec_len = record_ref.shape[1:]
    span = rec_len // DEC
    capacity = entries // windows
    stride = 2 * capacity
    width = taps.shape[1]
    copies = [
        pltpu.make_async_copy(source, target, arrivals.at[index])
        for index, (source, target) in enumerate(
            [
                (band_hbm, band_ref),
                (window_hbm, window_ref),
                (start_hbm, start_ref),
                (live_hbm, live_ref),
                (record_hbm, record_ref),
            ]
        )
    ]
    for copy in copies:
        copy.start()

    for copy in copies[:4]:
        copy.wait()
    taps[...] = jnp.zeros_like(taps)
    taps[0:1, 0:TAPS] = band_ref[...].reshape(1, TAPS)
    base = jnp.broadcast_to(taps[0:1, :], taps.shape)
    firsts = list(range(HEAD, HEAD + span, 8)) + [0, span, 0, span, 0]
    bands = [
        pltpu.roll(base, (DEC * first - DEC * HEAD) % width, 1, stride=DEC, stride_axis=0)[:, :rec_len]
        for first in firsts
    ]
    bands.append(jnp.zeros((LANES - 8 * len(firsts), rec_len), F32))
    filters = jnp.concatenate(bands, 0)
    window = window_ref[...]
    label = start_ref[...] // rec_len
    channel = label // slots
    slot = label - channel * slots
    labels[...] = jnp.zeros_like(labels)
    mark = span + 5 * HEAD
    labels[mark : mark + 1, 0:entries] = (slot + 1).astype(F32)
    labels[mark + 1 : mark + 2, 0:entries] = row_of(channel).astype(F32)
    marks = labels[...].T[:entries]
    live = lane_of((1, entries)) < live_ref[0, 0]
    each = lax.broadcasted_iota(jnp.int32, (windows, entries), 0)
    member = (window == each) & live
    ahead = (window == each + 1) & live & (slot < 3)
    both = jnp.concatenate([jnp.where(member, 1.0, 0.0), jnp.where(ahead, 1.0, 0.0)], 0)
    before = lax.broadcasted_iota(jnp.int32, (entries, entries), 0) <= lane_of((entries, entries))
    count = jnp.dot(both.astype(BF), jnp.where(before, 1.0, 0.0).astype(BF), preferred_element_type=F32)
    first = (each * stride).astype(F32)
    place = jnp.sum(jnp.where(member, count[:windows] + first, 0.0), 0, keepdims=True) - 1.0
    place_ahead = (
        jnp.sum(jnp.where(ahead, count[windows:] + (first + capacity), 0.0), 0, keepdims=True) - 1.0
    )
    copies[4].wait()
    value = lax.dot_general(
        record_ref[0],
        filters,
        (((1,), (1,)), ((), ())),
        precision=lax.Precision.HIGHEST,
        preferred_element_type=F32,
    )
    high = value.astype(BF).astype(F32)
    rest = value - high
    middle = rest.astype(BF).astype(F32)
    low = rest - middle

    lane = lane_of(value.shape)
    payload = jnp.where(
        lane < span + HEAD,
        high,
        jnp.where(lane < span + 3 * HEAD, middle, jnp.where(lane < mark, low, marks)),
    ).astype(BF)

    total = out_ref.shape[0]
    part = total // 4
    for index in range(4):
        row = (lax.broadcasted_iota(jnp.int32, (part, entries), 0) + index * part).astype(F32)
        chosen = jnp.where((row == place) | (row == place_ahead), 1.0, 0.0).astype(BF)
        out_ref[index * part : (index + 1) * part, :] = jnp.dot(
            chosen, payload, preferred_element_type=F32
        ).astype(BF)


def pack(records, band_filter, windows_of, starts, live, slots, windows):
    entries, rec_len = records.shape[1:]
    return pl.pallas_call(
        functools.partial(pack_kernel, slots, windows),
        out_shape=jax.ShapeDtypeStruct((2 * entries, LANES), BF),
        in_specs=[whole(pltpu.HBM)] * 5,
        out_specs=whole(),
        scratch_shapes=[
            pltpu.SMEM(live.shape, live.dtype),
            pltpu.VMEM(records.shape, F32),
            pltpu.VMEM(band_filter.shape, F32),
            pltpu.VMEM(windows_of.shape, windows_of.dtype),
            pltpu.VMEM(starts.shape, starts.dtype),
            pltpu.VMEM((8, rec_len + LANES), F32),
            pltpu.VMEM((LANES, pl.cdiv(entries, LANES) * LANES), F32),
            pltpu.SemaphoreType.DMA((5,)),
        ],
        compiler_params=pltpu.CompilerParams(vmem_limit_bytes=60 * MIB),
    )(live, records, band_filter, windows_of, starts)


def arrange_kernel(slots, stride, arrived_ref, after_ref, out_ref):
    del after_ref
    total = arrived_ref.shape[0]
    rows = out_ref.shape[1]
    blocks = out_ref.shape[0] - 1
    span = LANES // 2
    mark = span + 5 * HEAD
    arrived = arrived_ref[...]
    lane = lane_of((8, LANES))
    weigh = jnp.where(lane == mark, float(rows), jnp.where(lane == mark + 1, 1.0, 0.0)).astype(BF)
    name = lax.dot_general(weigh, arrived, (((1,), (1,)), ((), ())), preferred_element_type=F32)[0:1]
    ahead = lane_of((1, total)) % stride >= stride // 2
    target = jnp.where(name > 0, name - rows + jnp.where(ahead, float(slots * rows), 0.0), -1.0)
    held = slots + 3
    row = lax.broadcasted_iota(jnp.int32, (held * rows, total), 0).astype(F32)
    chosen = jnp.where(row == target, 1.0, 0.0).astype(BF)
    placed = jnp.dot(chosen, arrived, preferred_element_type=F32)
    lane = lane_of((rows, LANES))
    own = []
    previous = None
    for slot in range(held):
        part = placed[slot * rows : (slot + 1) * rows]
        summed = (
            part
            + pltpu.roll(part, LANES - 2 * HEAD, 1)
            + pltpu.roll(part, LANES - 4 * HEAD, 1)
        )
        if previous is not None:
            kept, tail = previous
            tail = tail + pltpu.roll(summed, LANES - HEAD, 1)
            own.append(jnp.where(lane < span - HEAD, kept, tail))
        previous = part, summed
    pairs = []
    for index in range(0, slots + 2, 2):
        pairs.append(jnp.where(lane < span, own[index], pltpu.roll(own[index + 1], span, 1)))
    turned = turn(pairs[:blocks])
    for index, value in enumerate(turned + pairs[blocks:]):
        out_ref[index] = flip(value).astype(BF)


def arrange(arrived, after, slots, stride, rows):
    total = arrived.shape[0]
    return pl.pallas_call(
        functools.partial(arrange_kernel, slots, stride),
        out_shape=jax.ShapeDtypeStruct((slots // 2 + 1, rows, LANES), BF),
        in_specs=[whole(), whole(pl.ANY)],
        out_specs=whole(),
        compiler_params=pltpu.CompilerParams(vmem_limit_bytes=50 * MIB),
    )(arrived, after)


def regroup_kernel(template_hbm, out_hbm, held, turned, arrivals, departures):
    kept, channels = template_hbm.shape[:2]

    def fetch(index):
        part = pl.ds(CHUNK * index, CHUNK)
        return pltpu.make_async_copy(template_hbm.at[:, part, :], held.at[:, part, :], arrivals.at[index])

    def send(index):
        part = pl.ds(CHUNK * index, CHUNK)
        return pltpu.make_async_copy(turned.at[part], out_hbm.at[part], departures.at[index])

    parts = channels // CHUNK
    for index in range(parts):
        fetch(index).start()

    def one_part(index, carry):
        fetch(index).wait()
        part = pl.ds(CHUNK * index, CHUNK)
        for first in range(0, kept, CHUNK):
            rows = slice(first, first + CHUNK)
            turned[part, rows, :] = jnp.swapaxes(held[rows, part, :], 0, 1)
        send(index).start()
        return carry

    lax.fori_loop(0, parts, one_part, 0)
    for index in range(parts):
        send(index).wait()


def regroup(templates):
    kept, channels, tlen = templates.shape
    turned = (channels, kept, tlen)
    return pl.pallas_call(
        regroup_kernel,
        in_specs=[whole(pltpu.HBM)],
        out_specs=whole(pltpu.HBM),
        out_shape=jax.ShapeDtypeStruct(turned, BF),
        scratch_shapes=[
            pltpu.VMEM(templates.shape, BF),
            pltpu.VMEM(turned, BF),
            pltpu.SemaphoreType.DMA((channels // CHUNK,)),
            pltpu.SemaphoreType.DMA((channels // CHUNK,)),
        ],
        compiler_params=pltpu.CompilerParams(vmem_limit_bytes=56 * MIB),
        cost_estimate=pl.CostEstimate(flops=2 * templates.size, bytes_accessed=4 * templates.size, transcendentals=0),
    )(templates)


def shifted(here, there, row, out):
    step = lax.broadcasted_iota(jnp.int32, (8, LANES), 0)
    within = lane_of((8, LANES)) % CHUNK
    blocks = out.shape[1] // CHUNK
    for side in range(2):
        for block in range(blocks):
            one = jnp.broadcast_to(here[block, pl.ds(row + side, 1), :], (8, LANES))
            other = jnp.broadcast_to(there[block + 1, pl.ds(row + side, 1), :], (8, LANES))
            halves = [
                pltpu.roll(jnp.where(within < CHUNK - first - step, one, other), first, 1, stride=1, stride_axis=0)
                for first in (0, 8)
            ]
            out[side, CHUNK * block : CHUNK * (block + 1), :] = jnp.concatenate(halves, 0).astype(BF)


def correlate_kernel(steps, begun, *refs):
    refs = list(refs)
    sample_refs = [refs.pop(0) for _ in steps]
    template_hbm = refs.pop(0)
    begun_refs = [refs.pop(0) for _ in range(3 if begun else 0)]
    out_refs = [refs.pop(0) for _ in range(1 if begun else 3)]
    samples, held, *unfolded, even, odd, power, square, total, arrivals, template_arrivals, departures = refs
    unfolded = unfolded[:2], unfolded[2:]
    blocks, rows = samples.shape[1:3]
    blocks -= 1
    count, channels, kept, tlen = held.shape
    pairs = channels // 2
    me = lax.axis_index("tmpl")
    norm = float(CH * tlen)
    lane = lane_of((1, LANES))

    fetches = [
        pltpu.make_async_copy(source, samples.at[index], arrivals.at[index])
        for index, source in enumerate(sample_refs)
    ]
    for fetch in fetches:
        fetch.start()

    def fetch_templates(index):
        first = (me ^ steps[index]) * channels
        return pltpu.make_async_copy(
            template_hbm.at[pl.ds(first, channels)], held.at[index], template_arrivals.at[index]
        )

    for index in range(count):
        fetch_templates(index).start()

    def unfold(index, here, there, block):
        value = samples[index, block].astype(F32)
        after = samples[index, blocks].astype(F32)
        following = jnp.where(
            lane >= LANES - CHUNK,
            pltpu.roll(after, (LANES - CHUNK - CHUNK * block) % LANES, 1),
            pltpu.roll(value, LANES - CHUNK, 1),
        )
        here[block] = value
        here[block + blocks] = following
        there[block] = pltpu.roll(value, LANES - CHUNK, 1)
        there[block + blocks] = pltpu.roll(following, LANES - CHUNK, 1)
        power[block] += jnp.sum((value * value).reshape(rows // 8, 8, LANES), 0)
        if block == 0:
            power[blocks] += jnp.sum((after * after).reshape(rows // 8, 8, LANES), 0)

    def lag_scale():
        lines = [jnp.sum(power[block], 0, keepdims=True) for block in range(blocks + 1)]
        lines = turn(lines[:blocks]) + lines[blocks:]
        lines = [flip(jnp.broadcast_to(line, (8, LANES)))[0:1] for line in lines]
        later = jnp.concatenate(lines[:blocks], 0)
        earlier = jnp.concatenate(lines[1:], 0)
        step = 1
        while step < LANES:
            later = later + jnp.where(lane < LANES - step, pltpu.roll(later, LANES - step, 1), 0.0)
            earlier = earlier + jnp.where(lane >= step, pltpu.roll(earlier, step, 1), 0.0)
            step *= 2
        earlier = jnp.where(lane >= 1, pltpu.roll(earlier, 1, 1), 0.0)
        return lax.rsqrt((later + earlier) / norm + EPSILON) / norm

    def row_at(pair):
        return CHUNK * (2 * pair // GROUP) + 2 * pair % GROUP

    def products(*sums):
        if begun:
            power[...] = begun_refs[1][...]
            square[...] = begun_refs[2][...]
        else:
            power[...] = jnp.zeros_like(power)
            square[...] = jnp.zeros_like(square)
        fetches[0].wait()
        for block in range(blocks):
            unfold(0, *unfolded[0], block)
        shifted(*unfolded[0], 0, even)
        for fetch in fetches[1:]:
            fetch.wait()
        for index in range(count):
            side = index % 2
            fetch_templates(index).wait()
            for pair in range(pairs):
                now, then = (even, odd) if pair % 2 == 0 else (odd, even)
                taps = [held[index, 2 * pair + half] for half in range(2)]
                square[...] += sum(jnp.square(tap.astype(F32)) for tap in taps)
                taps = jnp.concatenate(taps, 1)
                for stage in range(2):
                    for unit in range(2):
                        first = 2 * (2 * unit + stage)
                        columns = [
                            jnp.concatenate(
                                [now[half, CHUNK * block : CHUNK * block + tlen, :] for half in range(2)], 0
                            )
                            for block in (first, first + 1)
                        ]
                        pltpu.matmul_push_rhs(jnp.concatenate(columns, 1), stage, unit)
                    for unit in range(2):
                        pltpu.matmul_acc_lhs(sums[2 * unit + stage], taps, load_staged_rhs=stage)
                if pair < blocks and index < count - 1:
                    unfold(index + 1, *unfolded[1 - side], pair)
                if pair < pairs - 1:
                    shifted(*unfolded[side], row_at(pair + 1), then)
                elif index < count - 1:
                    shifted(*unfolded[1 - side], 0, then)
        results = []
        for index, ref in enumerate(sums):
            value = pltpu.matmul_pop(ref)
            if begun:
                value = value + begun_refs[0][:, 2 * LANES * index : 2 * LANES * (index + 1)]
            results += [value[:, :LANES], value[:, LANES:]]
        if not begun:
            for block, value in enumerate(results):
                out_refs[0][:, LANES * block : LANES * (block + 1)] = value
            out_refs[1][...] = power[...]
            out_refs[2][...] = square[...]
            return
        scale = lag_scale()
        template_scale = lax.rsqrt(jnp.sum(square[...], 1, keepdims=True) / norm + EPSILON)
        height = kept // departures.shape[0]
        copies = []
        for part in range(departures.shape[0]):
            span = slice(part * height, (part + 1) * height)
            for block, value in enumerate(turn([result[span] for result in results])):
                total[span, LANES * block : LANES * (block + 1)] = (
                    flip(value) * template_scale[span] * scale[block : block + 1, :]
                )
            copies.append(pltpu.make_async_copy(total.at[span], out_refs[0].at[span], departures.at[part]))
            copies[-1].start()
        for copy in copies:
            copy.wait()

    pl.run_scoped(
        products, *[pltpu.ACC(unit)((kept, 2 * LANES), F32) for unit in (0, 0, 1, 1)]
    )


def correlate(steps, samples, templates, begun=()):
    channels, kept, tlen = templates.shape
    channels //= lax.axis_size("tmpl")
    blocks, rows = samples[0].shape[:2]
    blocks -= 1
    here = pltpu.VMEM((2 * blocks, rows, LANES), F32)
    shifts = pltpu.VMEM((2, CHUNK * (2 * blocks - 1), LANES), BF)
    result = jax.ShapeDtypeStruct((kept, blocks * LANES), F32)
    power = jax.ShapeDtypeStruct((blocks + 1, 8, LANES), F32)
    square = jax.ShapeDtypeStruct((kept, tlen), F32)
    count = len(steps)
    return pl.pallas_call(
        functools.partial(correlate_kernel, steps, bool(begun)),
        out_shape=result if begun else [result, power, square],
        in_specs=[whole(pl.ANY)] * count + [whole(pltpu.HBM)] + [whole()] * len(begun),
        out_specs=whole(pltpu.HBM) if begun else [whole()] * 3,
        scratch_shapes=[
            pltpu.VMEM((count, *samples[0].shape), BF),
            pltpu.VMEM((count, channels, kept, tlen), BF),
            *[here] * 4,
            shifts,
            shifts,
            pltpu.VMEM(power.shape, F32),
            pltpu.VMEM(square.shape, F32),
            pltpu.VMEM(result.shape if begun else (8, LANES), F32),
            pltpu.SemaphoreType.DMA((count,)),
            pltpu.SemaphoreType.DMA((count,)),
            pltpu.SemaphoreType.DMA((4,)),
        ],
        compiler_params=pltpu.CompilerParams(vmem_limit_bytes=50 * MIB),
        cost_estimate=pl.CostEstimate(
            flops=2 * kept * blocks * LANES * count * channels * tlen,
            bytes_accessed=2 * count * channels * kept * tlen,
            transcendentals=0,
        ),
    )(*samples, templates, *begun)


def shards(records, band_filter, templates, destinations, offsets, live_counts):
    windows = lax.axis_size("tm")
    quarters = lax.axis_size("tmpl")
    entries, rec_len = records.shape[1:]
    channels = CH // quarters
    slots = entries // channels
    stride = 2 * (entries // windows)
    rows = channels // GROUP * CHUNK
    outgoing = pack(records, band_filter, destinations, offsets, live_counts, slots, windows)
    outgoing = outgoing.reshape(windows, stride, LANES)
    arrived = lax.all_to_all(outgoing, "tm", split_axis=0, concat_axis=0, tiled=True)
    grouped = regroup(templates)
    own = arrange(arrived.reshape(2 * entries, LANES), grouped, slots, stride, rows)
    steps = tuple(range(1, quarters))
    samples = [
        lax.ppermute(own, "tmpl", [(source, source ^ step) for source in range(quarters)]) for step in steps
    ]
    begun = correlate((0,), [own], grouped)
    return correlate(steps, samples, grouped, begun)


def solution(mesh):
    in_specs = (
        P("tmpl", "tm", None),
        P(),
        P("tmpl", None, None),
        P("tmpl", "tm"),
        P("tmpl", "tm"),
        P("tmpl", "tm"),
    )
    out_specs = P("tmpl", "tm")
    inner = jax.shard_map(shards, mesh=mesh, in_specs=in_specs, out_specs=out_specs, check_vma=False)
    return inner
```

time: 57.3 us -> 43.9 us (0.77)
  local copies, waits for them, and re-layouts: 10.6 us -> 0 us
  blocking collectives: 6.76 us -> 0 us
  waiting for transfers between devices: 0.01 us -> 3.33 us
  starting transfers between devices: 7.25 us -> 9.18 us
  Pallas kernels: 31.6 us -> 30.2 us
    unnamed x12 -> x0, local copies, waits for them, and re-layouts: 10.6 us -> none
    all_gather x1 -> x0, blocking collectives: 6.76 us -> none  [shards(): samples = lax.all_gather(samples, 'tmpl', axis=0, tiled=False)]
    pallas_call x2 -> x3, Pallas kernels: 26.8 us -> 24.3 us  [the longest x2 16.7 us: correlate(): pl.pallas_call(functools.partial(correlate_kernel, steps, bool(begun)), o...]
    all_to_all x1, waiting for transfers between devices: 0.01 us -> 2.01 us  [shards(): lax.all_to_all(outgoing, 'tm', split_axis=0, concat_axis=0, tiled=True)]
    ppermute x0 -> x3, starting transfers between devices: none -> 1.92 us  [shards(): lax.ppermute(own, 'tmpl', [(source, source ^ step) for source in range(qu...]
    ppermute x0 -> x3, waiting for transfers between devices: none -> 1.32 us  [shards(): lax.ppermute(own, 'tmpl', [(source, source ^ step) for source in range(qu...]
    pallas_call x1, Pallas kernels: 3.26 us -> 4.35 us  [pack(): pl.pallas_call(functools.partial(pack_kernel, slots, windows), out_shape=...]
  transfers between devices with their start and end apart: 1 -> 4, of which waited for: 0 -> 2; matrix products, arithmetic and copies ran while one was open for 0% -> 0% of each run, Pallas kernels for 19% -> 28%
where the time goes in v2:
time: 43.9 us; the launch traced here: 43.6 us
  Pallas kernels  30.2 us (69%)
  starting transfers between devices  9.18 us (21%)
  waiting for transfers between devices  3.33 us (8%)
  between operations  0.86 us (2%)
    pallas_call x2, Pallas kernels, correlate(): pl.pallas_call(functools.partial(correlate_kernel, steps, bool(begun)), o...  16.7 us
    pallas_call x1, Pallas kernels, regroup(): pl.pallas_call(regroup_kernel, in_specs=[whole(pltpu.HBM)], out_specs=who...  7.6 us
    all_to_all x1, starting transfers between devices, shards(): lax.all_to_all(outgoing, 'tm', split_axis=0, concat_axis=0, tiled=True)  7.27 us
    pallas_call x1, Pallas kernels, pack(): pl.pallas_call(functools.partial(pack_kernel, slots, windows), out_shape=...  4.35 us
    all_to_all x1, waiting for transfers between devices, shards(): lax.all_to_all(outgoing, 'tm', split_axis=0, concat_axis=0, tiled=True)  2.01 us
    ppermute x3, starting transfers between devices, shards(): lax.ppermute(own, 'tmpl', [(source, source ^ step) for source in range(qu...  1.92 us
    pallas_call x1, Pallas kernels, arrange(): pl.pallas_call(functools.partial(arrange_kernel, slots, stride), out_shap...  1.57 us
    ppermute x3, waiting for transfers between devices, shards(): lax.ppermute(own, 'tmpl', [(source, source ^ step) for source in range(qu...  1.32 us
  transfers between devices with their start and end apart: 4, of which 2 were waited for; matrix products, arithmetic and copies ran while one was open for 0% of the time, Pallas kernels for 28%

profile of v2, /device:TPU:0, one launch (start us, length us, event | category | flops | bytes accessed | tf_op | source)
XLA Modules:
  0.0 43.6 jit_solution(14999526137155319469)
XLA Ops:
  0.7 4.3 %shard_map.64 = bf16[1152,128]{1,0:T(8,128)(2,1)} custom-call(s32[1,1]{1,0:T(1,128)S(6)} %copy.7.live_hbm, f32[1,576,512]{2,1,0:T(8,128)} %record_hbm.1, f32[65]{0:T(128)} %band_hbm.1, s32[1,576]{1,0:T(1,128)} %window_hbm.1, s32[1,576]{1,0:T(1,128)} %start_hbm.1), custom_call_target="tpu_custom_call" | custom-call | tf_op jit(solution)/shard_map/pallas_call | solution.py:164
  5.0 7.3 %all-to-all-start = ((bf16[8,144,128]{2,1,0:T(8,128)(2,1)}), bf16[8,144,128]{2,1,0:T(8,128)(2,1)S(1)}, u32[]{:S(2)}, u32[]{:S(2)}) async-start(bf16[8,144,128]{2,1,0:T(8,128)(2,1)} %bitcast.3), calls=%async_computation | async-start | bytes 589824 | tf_op jit(solution)/shard_map/all_to_all | solution.py:481
  12.3 7.6 %shard_map.65.after_ref.refs_1_.refs_3_ = bf16[144,256,128]{2,1,0:T(8,128)(2,1)} custom-call(bf16[256,144,128]{2,1,0:T(8,128)(2,1)} %template_hbm.1), custom_call_target="tpu_custom_call" | custom-call | flops 9437184 | bytes 18874368 | tf_op jit(solution)/shard_map/pallas_call | solution.py:266
  19.9 2.0 %all-to-all-done = bf16[8,144,128]{2,1,0:T(8,128)(2,1)S(1)} async-done(((bf16[8,144,128]{2,1,0:T(8,128)(2,1)}), bf16[8,144,128]{2,1,0:T(8,128)(2,1)S(1)}, u32[]{:S(2)}, u32[]{:S(2)}) %all-to-all-start) | async-done | bytes 294944 | tf_op jit(solution)/shard_map/all_to_all | solution.py:481
  21.9 1.6 %shard_map.66.refs_0_ = bf16[9,48,128]{2,1,0:T(8,128)(2,1)S(1)} custom-call(bf16[1152,128]{1,0:T(8,128)(2,1)S(1)} %bitcast.2, bf16[144,256,128]{2,1,0:T(8,128)(2,1)} %shard_map.65.after_ref.refs_1_.refs_3_), custom_call_target="tpu_custom_call" | custom-call | tf_op jit(solution)/shard_map/pallas_call | solution.py:225
  23.5 0.1 collective-permute-start.2
  23.5 1.6 %collective-permute-start.1 = (bf16[9,48,128]{2,1,0:T(8,128)(2,1)S(1)}, bf16[9,48,128]{2,1,0:T(8,128)(2,1)S(1)}, u32[]{:S(2)}, u32[]{:S(2)}) collective-permute-start(bf16[9,48,128]{2,1,0:T(8,128)(2,1)S(1)} %shard_map.66.refs_0_), channel_id=1, source_target_pairs={{0,2},{1,3},{2,0},{3,1},{4,6},{5,7},{6,4},{7,5},{8,10},{9,11},{10,... | collective-permute-start | bytes 331784 | tf_op jit(solution)/shard_map/ppermute | solution.py:486
  25.1 0.3 collective-permute-start
  25.4 4.5 %shard_map.67 = (f32[256,1024]{1,0:T(8,128)S(1)}, f32[9,8,128]{2,1,0:T(8,128)S(1)}, f32[256,128]{1,0:T(8,128)S(1)}) custom-call(bf16[9,48,128]{2,1,0:T(8,128)(2,1)S(1)} %shard_map.66.refs_0_, bf16[144,256,128]{2,1,0:T(8,128)(2,1)} %shard_map.65.after_ref.refs_1_.refs_3_), custom_call_target="tpu_custom_call" | custom-call | flops 2415919104 | bytes 2359296 | tf_op jit(solution)/shard_map/pallas_call | solution.py:444
  29.9 0.0 collective-permute-done.2.refs_2_
  29.9 1.3 %collective-permute-done.1.refs_1_ = bf16[9,48,128]{2,1,0:T(8,128)(2,1)S(1)} collective-permute-done((bf16[9,48,128]{2,1,0:T(8,128)(2,1)S(1)}, bf16[9,48,128]{2,1,0:T(8,128)(2,1)S(1)}, u32[]{:S(2)}, u32[]{:S(2)}) %collective-permute-start.1) | collective-permute-done | bytes 110624 | tf_op jit(solution)/shard_map/ppermute | solution.py:486
  31.3 0.0 collective-permute-done.refs_0_
  31.3 12.2 %shard_map.68 = f32[256,1024]{1,0:T(8,128)} custom-call(bf16[9,48,128]{2,1,0:T(8,128)(2,1)S(1)} %collective-permute-done.refs_0_, bf16[9,48,128]{2,1,0:T(8,128)(2,1)S(1)} %collective-permute-done.1.refs_1_, bf16[9,48,128]{2,1,0:T(8,128)(2,1)S(1)} %collective-permute-done.2.refs_2_, bf16[144,256,128]{2,1,0:T(8,128)(2,1)} %shard_map.65.after_ref.refs_1_.refs_3_, ...), custom_call_target="tpu_custom_call" | custom-call | flops 7247757312 | bytes 7077888 | tf_op jit(solution)/shard_map/pallas_call | solution.py:444
Async XLA Ops:
  5.0 16.9 %all-to-all-start = ((bf16[8,144,128]{2,1,0:T(8,128)(2,1)}), bf16[8,144,128]{2,1,0:T(8,128)(2,1)S(1)}, u32[]{:S(2)}, u32[]{:S(2)}) async-start(bf16[8,144,128]{2,1,0:T(8,128)(2,1)} %bitcast.3), calls=%async_computation | async-start | bytes 589824 | tf_op jit(solution)/shard_map/all_to_all | solution.py:481
  23.5 6.5 %collective-permute-start.2 = (bf16[9,48,128]{2,1,0:T(8,128)(2,1)S(1)}, bf16[9,48,128]{2,1,0:T(8,128)(2,1)S(1)}, u32[]{:S(2)}, u32[]{:S(2)}) collective-permute-start(bf16[9,48,128]{2,1,0:T(8,128)(2,1)S(1)} %shard_map.66.refs_0_), channel_id=1, source_target_pairs={{0,3},{1,2},{2,1},{3,0},{4,7},{5,6},{6,5},{7,4},{8,11},{9,10},{10,... | collective-permute-start | bytes 331784 | tf_op jit(solution)/shard_map/ppermute | solution.py:486
  23.5 7.7 %collective-permute-start.1 = (bf16[9,48,128]{2,1,0:T(8,128)(2,1)S(1)}, bf16[9,48,128]{2,1,0:T(8,128)(2,1)S(1)}, u32[]{:S(2)}, u32[]{:S(2)}) collective-permute-start(bf16[9,48,128]{2,1,0:T(8,128)(2,1)S(1)} %shard_map.66.refs_0_), channel_id=1, source_target_pairs={{0,2},{1,3},{2,0},{3,1},{4,6},{5,7},{6,4},{7,5},{8,10},{9,11},{10,... | collective-permute-start | bytes 331784 | tf_op jit(solution)/shard_map/ppermute | solution.py:486
  25.1 6.1 %collective-permute-start = (bf16[9,48,128]{2,1,0:T(8,128)(2,1)S(1)}, bf16[9,48,128]{2,1,0:T(8,128)(2,1)S(1)}, u32[]{:S(2)}, u32[]{:S(2)}) collective-permute-start(bf16[9,48,128]{2,1,0:T(8,128)(2,1)S(1)} %shard_map.66.refs_0_), channel_id=1, source_target_pairs={{0,1},{1,0},{2,3},{3,2},{4,5},{5,4},{6,7},{7,6},{8,9},{9,8},{10,11... | collective-permute-start | bytes 331784 | tf_op jit(solution)/shard_map/ppermute | solution.py:486

commit v3 on v2

--- a/solution.py
+++ b/solution.py
@@ -15,7 +15,6 @@
 LANES = 128
 CHUNK = 16
 HEAD = (TAPS - 1) // DEC
-GROUP = 12
 MIB = 2**20
 BF = jnp.bfloat16
 F32 = jnp.float32
@@ -27,13 +26,6 @@
 
 def lane_of(shape):
     return lax.broadcasted_iota(jnp.int32, shape, len(shape) - 1)
-
-
-def row_of(channel):
-    row = channel
-    for first in range(GROUP, CH, GROUP):
-        row = row + jnp.where(channel >= first, CHUNK - GROUP, 0)
-    return row
 
 
 def flip(values):
@@ -74,6 +66,7 @@
     start_ref,
     taps,
     labels,
+    before,
     arrivals,
 ):
     entries, rec_len = record_ref.shape[1:]
@@ -96,9 +89,13 @@
     for copy in copies:
         copy.start()
 
+    before[...] = jnp.where(
+        lax.broadcasted_iota(jnp.int32, before.shape, 0) <= lane_of(before.shape), 1.0, 0.0
+    ).astype(BF)
+    taps[...] = jnp.zeros_like(taps)
+    labels[...] = jnp.zeros_like(labels)
     for copy in copies[:4]:
         copy.wait()
-    taps[...] = jnp.zeros_like(taps)
     taps[0:1, 0:TAPS] = band_ref[...].reshape(1, TAPS)
     base = jnp.broadcast_to(taps[0:1, :], taps.shape)
     firsts = list(range(HEAD, HEAD + span, 8)) + [0, span, 0, span, 0]
@@ -108,40 +105,42 @@
     ]
     bands.append(jnp.zeros((LANES - 8 * len(firsts), rec_len), F32))
     filters = jnp.concatenate(bands, 0)
+    filter_high = filters.astype(BF)
+    filter_low = (filters - filter_high.astype(F32)).astype(BF)
+    filters = jnp.concatenate([filter_high, filter_low], 0)
+
     window = window_ref[...]
     label = start_ref[...] // rec_len
     channel = label // slots
     slot = label - channel * slots
-    labels[...] = jnp.zeros_like(labels)
     mark = span + 5 * HEAD
     labels[mark : mark + 1, 0:entries] = (slot + 1).astype(F32)
-    labels[mark + 1 : mark + 2, 0:entries] = row_of(channel).astype(F32)
+    labels[mark + 1 : mark + 2, 0:entries] = channel.astype(F32)
     marks = labels[...].T[:entries]
     live = lane_of((1, entries)) < live_ref[0, 0]
     each = lax.broadcasted_iota(jnp.int32, (windows, entries), 0)
     member = (window == each) & live
     ahead = (window == each + 1) & live & (slot < 3)
     both = jnp.concatenate([jnp.where(member, 1.0, 0.0), jnp.where(ahead, 1.0, 0.0)], 0)
-    before = lax.broadcasted_iota(jnp.int32, (entries, entries), 0) <= lane_of((entries, entries))
-    count = jnp.dot(both.astype(BF), jnp.where(before, 1.0, 0.0).astype(BF), preferred_element_type=F32)
+    count = jnp.dot(both.astype(BF), before[...], preferred_element_type=F32)
     first = (each * stride).astype(F32)
     place = jnp.sum(jnp.where(member, count[:windows] + first, 0.0), 0, keepdims=True) - 1.0
     place_ahead = (
         jnp.sum(jnp.where(ahead, count[windows:] + (first + capacity), 0.0), 0, keepdims=True) - 1.0
     )
+
     copies[4].wait()
-    value = lax.dot_general(
-        record_ref[0],
-        filters,
-        (((1,), (1,)), ((), ())),
-        precision=lax.Precision.HIGHEST,
-        preferred_element_type=F32,
-    )
+    contract = (((1,), (1,)), ((), ()))
+    record = record_ref[0]
+    record_high = record.astype(BF)
+    record_low = (record - record_high.astype(F32)).astype(BF)
+    upper = lax.dot_general(record_high, filters, contract, preferred_element_type=F32)
+    lower = lax.dot_general(record_low, filters, contract, preferred_element_type=F32)
+    value = upper[:, :LANES] + (upper[:, LANES:] + (lower[:, :LANES] + lower[:, LANES:]))
     high = value.astype(BF).astype(F32)
     rest = value - high
     middle = rest.astype(BF).astype(F32)
     low = rest - middle
-
     lane = lane_of(value.shape)
     payload = jnp.where(
         lane < span + HEAD,
@@ -150,12 +149,23 @@
     ).astype(BF)
 
     total = out_ref.shape[0]
-    part = total // 4
-    for index in range(4):
-        row = (lax.broadcasted_iota(jnp.int32, (part, entries), 0) + index * part).astype(F32)
-        chosen = jnp.where((row == place) | (row == place_ahead), 1.0, 0.0).astype(BF)
+    plain = capacity % 8 == 0
+    part = stride if plain else total // 4
+    row = lax.broadcasted_iota(jnp.int32, (part, entries), 0).astype(F32)
+    for index in range(total // part):
+        here, there = place - float(index * part), place_ahead - float(index * part)
+        if plain:
+            chosen = jnp.concatenate(
+                [
+                    jnp.where(row[:capacity] == here, 1.0, 0.0),
+                    jnp.where(row[capacity:] == there, 1.0, 0.0),
+                ],
+                0,
+            )
+        else:
+            chosen = jnp.where((row == here) | (row == there), 1.0, 0.0)
         out_ref[index * part : (index + 1) * part, :] = jnp.dot(
-            chosen, payload, preferred_element_type=F32
+            chosen.astype(BF), payload, preferred_element_type=F32
         ).astype(BF)
 
 
@@ -174,29 +184,41 @@
             pltpu.VMEM(starts.shape, starts.dtype),
             pltpu.VMEM((8, rec_len + LANES), F32),
             pltpu.VMEM((LANES, pl.cdiv(entries, LANES) * LANES), F32),
+            pltpu.VMEM((entries, entries), BF),
             pltpu.SemaphoreType.DMA((5,)),
         ],
         compiler_params=pltpu.CompilerParams(vmem_limit_bytes=60 * MIB),
     )(live, records, band_filter, windows_of, starts)
 
 
-def arrange_kernel(slots, stride, arrived_ref, after_ref, out_ref):
-    del after_ref
+def arrange_kernel(slots, stride, arrived_ref, template_hbm, out_ref, held_ref, arrival):
+    fetch = pltpu.make_async_copy(template_hbm.at[: held_ref.shape[0]], held_ref, arrival)
+    fetch.start()
     total = arrived_ref.shape[0]
-    rows = out_ref.shape[1]
-    blocks = out_ref.shape[0] - 1
+    channels = out_ref.shape[0]
+    rows = pl.cdiv(channels, 8) * 8
+    blocks = out_ref.shape[1] // LANES - 1
     span = LANES // 2
     mark = span + 5 * HEAD
-    arrived = arrived_ref[...]
+    arrived = arrived_ref[...].astype(F32)
+    capacity = stride // 2
     lane = lane_of((8, LANES))
     weigh = jnp.where(lane == mark, float(rows), jnp.where(lane == mark + 1, 1.0, 0.0)).astype(BF)
-    name = lax.dot_general(weigh, arrived, (((1,), (1,)), ((), ())), preferred_element_type=F32)[0:1]
-    ahead = lane_of((1, total)) % stride >= stride // 2
-    target = jnp.where(name > 0, name - rows + jnp.where(ahead, float(slots * rows), 0.0), -1.0)
+    placed = []
+    for side, count in enumerate((slots, 3)):
+        values = jnp.concatenate(
+            [
+                arrived[first : first + capacity]
+                for first in range(side * capacity, total, stride)
+            ],
+            0,
+        ).astype(BF)
+        name = lax.dot_general(weigh, values, (((1,), (1,)), ((), ())), preferred_element_type=F32)[0:1]
+        row = lax.broadcasted_iota(jnp.int32, (count * rows, total // 2), 0).astype(F32)
+        chosen = jnp.where(row == name - float(rows), 1.0, 0.0).astype(BF)
+        placed.append(jnp.dot(chosen, values, preferred_element_type=F32))
+    placed = jnp.concatenate(placed, 0)
     held = slots + 3
-    row = lax.broadcasted_iota(jnp.int32, (held * rows, total), 0).astype(F32)
-    chosen = jnp.where(row == target, 1.0, 0.0).astype(BF)
-    placed = jnp.dot(chosen, arrived, preferred_element_type=F32)
     lane = lane_of((rows, LANES))
     own = []
     previous = None
@@ -217,47 +239,57 @@
         pairs.append(jnp.where(lane < span, own[index], pltpu.roll(own[index + 1], span, 1)))
     turned = turn(pairs[:blocks])
     for index, value in enumerate(turned + pairs[blocks:]):
-        out_ref[index] = flip(value).astype(BF)
-
-
-def arrange(arrived, after, slots, stride, rows):
-    total = arrived.shape[0]
+        out_ref[:, LANES * index : LANES * (index + 1)] = flip(value)[:channels].astype(BF)
+    fetch.wait()
+
+
+def arrange(arrived, templates, slots, stride, channels):
     return pl.pallas_call(
         functools.partial(arrange_kernel, slots, stride),
-        out_shape=jax.ShapeDtypeStruct((slots // 2 + 1, rows, LANES), BF),
-        in_specs=[whole(), whole(pl.ANY)],
-        out_specs=whole(),
+        out_shape=[
+            jax.ShapeDtypeStruct((channels, (slots // 2 + 1) * LANES), BF),
+            jax.ShapeDtypeStruct((channels // 3, *templates.shape[1:]), BF),
+        ],
+        in_specs=[whole(), whole(pltpu.HBM)],
+        out_specs=[whole(), whole()],
+        scratch_shapes=[pltpu.SemaphoreType.DMA],
         compiler_params=pltpu.CompilerParams(vmem_limit_bytes=50 * MIB),
-    )(arrived, after)
+    )(arrived, templates)
 
 
 def regroup_kernel(template_hbm, out_hbm, held, turned, arrivals, departures):
     kept, channels = template_hbm.shape[:2]
-
-    def fetch(index):
-        part = pl.ds(CHUNK * index, CHUNK)
-        return pltpu.make_async_copy(template_hbm.at[:, part, :], held.at[:, part, :], arrivals.at[index])
-
-    def send(index):
-        part = pl.ds(CHUNK * index, CHUNK)
-        return pltpu.make_async_copy(turned.at[part], out_hbm.at[part], departures.at[index])
-
-    parts = channels // CHUNK
-    for index in range(parts):
-        fetch(index).start()
-
-    def one_part(index, carry):
-        fetch(index).wait()
-        part = pl.ds(CHUNK * index, CHUNK)
-        for first in range(0, kept, CHUNK):
-            rows = slice(first, first + CHUNK)
-            turned[part, rows, :] = jnp.swapaxes(held[rows, part, :], 0, 1)
-        send(index).start()
-        return carry
-
-    lax.fori_loop(0, parts, one_part, 0)
-    for index in range(parts):
-        send(index).wait()
+    quarter = channels // lax.axis_size("tmpl")
+    parts = range(0, channels, CHUNK)
+
+    def fetch(first):
+        part = slice(first, first + CHUNK)
+        return pltpu.make_async_copy(template_hbm.at[:, part, :], held.at[:, part, :], arrivals.at[first // CHUNK])
+
+    fetches = [fetch(first) for first in parts]
+    for copy in fetches:
+        copy.start()
+    sends = []
+    for first, copy in zip(parts, fetches):
+        copy.wait()
+        for row in range(0, kept, CHUNK):
+            rows = slice(row, row + CHUNK)
+            turned[first : first + CHUNK, rows, :] = jnp.swapaxes(held[rows, first : first + CHUNK, :], 0, 1)
+        if first == 0:
+            me = lax.axis_index("tmpl")
+        edge = min((first // quarter + 1) * quarter, first + CHUNK)
+        for start, stop in ((first, edge), (edge, first + CHUNK)):
+            if start == stop:
+                continue
+            place = (me ^ (start // quarter)) * quarter + start % quarter
+            sends.append(
+                pltpu.make_async_copy(
+                    turned.at[start:stop], out_hbm.at[pl.ds(place, stop - start)], departures.at[len(sends)]
+                )
+            )
+            sends[-1].start()
+    for copy in sends:
+        copy.wait()
 
 
 def regroup(templates):
@@ -272,7 +304,7 @@
             pltpu.VMEM(templates.shape, BF),
             pltpu.VMEM(turned, BF),
             pltpu.SemaphoreType.DMA((channels // CHUNK,)),
-            pltpu.SemaphoreType.DMA((channels // CHUNK,)),
+            pltpu.SemaphoreType.DMA((channels // CHUNK + lax.axis_size("tmpl"),)),
         ],
         compiler_params=pltpu.CompilerParams(vmem_limit_bytes=56 * MIB),
         cost_estimate=pl.CostEstimate(flops=2 * templates.size, bytes_accessed=4 * templates.size, transcendentals=0),
@@ -296,39 +328,47 @@
 
 def correlate_kernel(steps, begun, *refs):
     refs = list(refs)
-    sample_refs = [refs.pop(0) for _ in steps]
+    samples = [refs.pop(0) for _ in steps]
     template_hbm = refs.pop(0)
+    first_ref = refs.pop(0)
     begun_refs = [refs.pop(0) for _ in range(3 if begun else 0)]
-    out_refs = [refs.pop(0) for _ in range(1 if begun else 3)]
-    samples, held, *unfolded, even, odd, power, square, total, arrivals, template_arrivals, departures = refs
+    out_refs = [refs.pop(0) for _ in range(1 if begun else 4)]
+    held, *unfolded, even, odd, power, square, total, arrivals, departures = refs
     unfolded = unfolded[:2], unfolded[2:]
-    blocks, rows = samples.shape[1:3]
-    blocks -= 1
-    count, channels, kept, tlen = held.shape
+    rows = samples[0].shape[0]
+    blocks = samples[0].shape[1] // LANES - 1
+    channels, kept, tlen = held.shape[1:]
     pairs = channels // 2
-    me = lax.axis_index("tmpl")
+    count = len(steps)
     norm = float(CH * tlen)
     lane = lane_of((1, LANES))
 
-    fetches = [
-        pltpu.make_async_copy(source, samples.at[index], arrivals.at[index])
-        for index, source in enumerate(sample_refs)
-    ]
-    for fetch in fetches:
-        fetch.start()
-
-    def fetch_templates(index):
-        first = (me ^ steps[index]) * channels
-        return pltpu.make_async_copy(
-            template_hbm.at[pl.ds(first, channels)], held.at[index], template_arrivals.at[index]
-        )
-
-    for index in range(count):
-        fetch_templates(index).start()
+    def fetch(start, stop, target, index):
+        return pltpu.make_async_copy(template_hbm.at[start:stop], target, arrivals.at[index])
+
+    early = first_ref.shape[0]
+    templates = [first_ref] + [held.at[index] for index in range(count - 1)]
+    if begun:
+        fetches = [
+            fetch(step * channels, (step + 1) * channels, held.at[index], index)
+            for index, step in enumerate(steps[1:])
+        ]
+    else:
+        fetches = [
+            fetch(early, channels, held.at[0, pl.ds(0, channels - early)], 0),
+            fetch(channels, 2 * channels, out_refs[3], 1),
+        ]
+    for copy in fetches if begun else fetches[:1]:
+        copy.start()
+
+    def taps_of(index, channel):
+        if not begun and channel >= early:
+            return held[0, channel - early]
+        return templates[index][channel]
 
     def unfold(index, here, there, block):
-        value = samples[index, block].astype(F32)
-        after = samples[index, blocks].astype(F32)
+        value = samples[index][:, LANES * block : LANES * (block + 1)].astype(F32)
+        after = samples[index][:, LANES * blocks :].astype(F32)
         following = jnp.where(
             lane >= LANES - CHUNK,
             pltpu.roll(after, (LANES - CHUNK - CHUNK * block) % LANES, 1),
@@ -338,12 +378,12 @@
         here[block + blocks] = following
         there[block] = pltpu.roll(value, LANES - CHUNK, 1)
         there[block + blocks] = pltpu.roll(following, LANES - CHUNK, 1)
-        power[block] += jnp.sum((value * value).reshape(rows // 8, 8, LANES), 0)
+        power[block : block + 1] += jnp.sum(value * value, 0, keepdims=True)
         if block == 0:
-            power[blocks] += jnp.sum((after * after).reshape(rows // 8, 8, LANES), 0)
+            power[blocks:] += jnp.sum(after * after, 0, keepdims=True)
 
     def lag_scale():
-        lines = [jnp.sum(power[block], 0, keepdims=True) for block in range(blocks + 1)]
+        lines = [power[block : block + 1] for block in range(blocks + 1)]
         lines = turn(lines[:blocks]) + lines[blocks:]
         lines = [flip(jnp.broadcast_to(line, (8, LANES)))[0:1] for line in lines]
         later = jnp.concatenate(lines[:blocks], 0)
@@ -356,9 +396,6 @@
         earlier = jnp.where(lane >= 1, pltpu.roll(earlier, 1, 1), 0.0)
         return lax.rsqrt((later + earlier) / norm + EPSILON) / norm
 
-    def row_at(pair):
-        return CHUNK * (2 * pair // GROUP) + 2 * pair % GROUP
-
     def products(*sums):
         if begun:
             power[...] = begun_refs[1][...]
@@ -366,18 +403,19 @@
         else:
             power[...] = jnp.zeros_like(power)
             square[...] = jnp.zeros_like(square)
-        fetches[0].wait()
         for block in range(blocks):
             unfold(0, *unfolded[0], block)
         shifted(*unfolded[0], 0, even)
-        for fetch in fetches[1:]:
-            fetch.wait()
         for index in range(count):
             side = index % 2
-            fetch_templates(index).wait()
+            if index > 0:
+                fetches[index - 1].wait()
             for pair in range(pairs):
                 now, then = (even, odd) if pair % 2 == 0 else (odd, even)
-                taps = [held[index, 2 * pair + half] for half in range(2)]
+                if not begun and 2 * pair == early:
+                    fetches[0].wait()
+                    fetches[1].start()
+                taps = [taps_of(index, 2 * pair + half) for half in range(2)]
                 square[...] += sum(jnp.square(tap.astype(F32)) for tap in taps)
                 taps = jnp.concatenate(taps, 1)
                 for stage in range(2):
@@ -395,7 +433,7 @@
                 if pair < blocks and index < count - 1:
                     unfold(index + 1, *unfolded[1 - side], pair)
                 if pair < pairs - 1:
-                    shifted(*unfolded[side], row_at(pair + 1), then)
+                    shifted(*unfolded[side], 2 * (pair + 1), then)
                 elif index < count - 1:
                     shifted(*unfolded[1 - side], 0, then)
         results = []
@@ -409,6 +447,7 @@
                 out_refs[0][:, LANES * block : LANES * (block + 1)] = value
             out_refs[1][...] = power[...]
             out_refs[2][...] = square[...]
+            fetches[1].wait()
             return
         scale = lag_scale()
         template_scale = lax.rsqrt(jnp.sum(square[...], 1, keepdims=True) / norm + EPSILON)
@@ -430,42 +469,41 @@
     )
 
 
-def correlate(steps, samples, templates, begun=()):
+def correlate(steps, samples, templates, first, begun=()):
     channels, kept, tlen = templates.shape
     channels //= lax.axis_size("tmpl")
-    blocks, rows = samples[0].shape[:2]
-    blocks -= 1
+    rows = samples[0].shape[0]
+    blocks = samples[0].shape[1] // LANES - 1
     here = pltpu.VMEM((2 * blocks, rows, LANES), F32)
     shifts = pltpu.VMEM((2, CHUNK * (2 * blocks - 1), LANES), BF)
     result = jax.ShapeDtypeStruct((kept, blocks * LANES), F32)
-    power = jax.ShapeDtypeStruct((blocks + 1, 8, LANES), F32)
+    power = jax.ShapeDtypeStruct((blocks + 1, LANES), F32)
     square = jax.ShapeDtypeStruct((kept, tlen), F32)
     count = len(steps)
+    held = (channels, kept, tlen)
     return pl.pallas_call(
         functools.partial(correlate_kernel, steps, bool(begun)),
-        out_shape=result if begun else [result, power, square],
-        in_specs=[whole(pl.ANY)] * count + [whole(pltpu.HBM)] + [whole()] * len(begun),
-        out_specs=whole(pltpu.HBM) if begun else [whole()] * 3,
+        out_shape=result if begun else [result, power, square, jax.ShapeDtypeStruct(held, BF)],
+        in_specs=[whole()] * count + [whole(pltpu.HBM)] + [whole()] * (1 + len(begun)),
+        out_specs=whole(pltpu.HBM) if begun else [whole()] * 4,
         scratch_shapes=[
-            pltpu.VMEM((count, *samples[0].shape), BF),
-            pltpu.VMEM((count, channels, kept, tlen), BF),
+            pltpu.VMEM((max(count - 1, 1), *held), BF),
             *[here] * 4,
             shifts,
             shifts,
             pltpu.VMEM(power.shape, F32),
             pltpu.VMEM(square.shape, F32),
             pltpu.VMEM(result.shape if begun else (8, LANES), F32),
-            pltpu.SemaphoreType.DMA((count,)),
-            pltpu.SemaphoreType.DMA((count,)),
+            pltpu.SemaphoreType.DMA((2,)),
             pltpu.SemaphoreType.DMA((4,)),
         ],
-        compiler_params=pltpu.CompilerParams(vmem_limit_bytes=50 * MIB),
+        compiler_params=pltpu.CompilerParams(vmem_limit_bytes=(50 if begun else 46) * MIB),
         cost_estimate=pl.CostEstimate(
             flops=2 * kept * blocks * LANES * count * channels * tlen,
             bytes_accessed=2 * count * channels * kept * tlen,
             transcendentals=0,
         ),
-    )(*samples, templates, *begun)
+    )(*samples, templates, first, *begun)
 
 
 def shards(records, band_filter, templates, destinations, offsets, live_counts):
@@ -475,18 +513,17 @@
     channels = CH // quarters
     slots = entries // channels
     stride = 2 * (entries // windows)
-    rows = channels // GROUP * CHUNK
     outgoing = pack(records, band_filter, destinations, offsets, live_counts, slots, windows)
     outgoing = outgoing.reshape(windows, stride, LANES)
     arrived = lax.all_to_all(outgoing, "tm", split_axis=0, concat_axis=0, tiled=True)
     grouped = regroup(templates)
-    own = arrange(arrived.reshape(2 * entries, LANES), grouped, slots, stride, rows)
+    own, first = arrange(arrived.reshape(2 * entries, LANES), grouped, slots, stride, channels)
     steps = tuple(range(1, quarters))
     samples = [
         lax.ppermute(own, "tmpl", [(source, source ^ step) for source in range(quarters)]) for step in steps
     ]
-    begun = correlate((0,), [own], grouped)
-    return correlate(steps, samples, grouped, begun)
+    *begun, first = correlate((0,), [own], grouped, first)
+    return correlate(steps, samples, grouped, first, begun)
 
 
 def solution(mesh):

time: 43.9 us -> 39.7 us (0.904)
  Pallas kernels: 30.2 us -> 26.7 us
  waiting for transfers between devices: 3.33 us -> 2.71 us
    pallas_call x2, Pallas kernels: 16.7 us -> 14.6 us  [correlate(): pl.pallas_call(functools.partial(correlate_kernel, steps, bool(begun)), o...]
    pallas_call x1, Pallas kernels: 4.35 us -> 3.18 us  [pack(): pl.pallas_call(functools.partial(pack_kernel, slots, windows), out_shape=...]
    ppermute x3, waiting for transfers between devices: 1.32 us -> 0.76 us  [shards(): lax.ppermute(own, 'tmpl', [(source, source ^ step) for source in range(qu...]
  transfers between devices with their start and end apart: 4 -> 4, of which waited for: 2 -> 2; matrix products, arithmetic and copies ran while one was open for 0% -> 0% of each run, Pallas kernels for 28% -> 30%
where the time goes in v3:
time: 39.7 us; the launch traced here: 39.4 us
  Pallas kernels  26.7 us (67%)
  starting transfers between devices  9.19 us (23%)
  waiting for transfers between devices  2.71 us (7%)
  between operations  0.86 us (2%)
    pallas_call x2, Pallas kernels, correlate(): pl.pallas_call(functools.partial(correlate_kernel, steps, bool(begun)), o...  14.6 us
    pallas_call x1, Pallas kernels, regroup(): pl.pallas_call(regroup_kernel, in_specs=[whole(pltpu.HBM)], out_specs=who...  7.65 us
    all_to_all x1, starting transfers between devices, shards(): lax.all_to_all(outgoing, 'tm', split_axis=0, concat_axis=0, tiled=True)  7.27 us
    pallas_call x1, Pallas kernels, pack(): pl.pallas_call(functools.partial(pack_kernel, slots, windows), out_shape=...  3.18 us
    all_to_all x1, waiting for transfers between devices, shards(): lax.all_to_all(outgoing, 'tm', split_axis=0, concat_axis=0, tiled=True)  1.96 us
    ppermute x3, starting transfers between devices, shards(): lax.ppermute(own, 'tmpl', [(source, source ^ step) for source in range(qu...  1.92 us
    pallas_call x1, Pallas kernels, arrange(): pl.pallas_call(functools.partial(arrange_kernel, slots, stride), out_shap...  1.22 us
  transfers between devices with their start and end apart: 4, of which 2 were waited for; matrix products, arithmetic and copies ran while one was open for 0% of the time, Pallas kernels for 30%

profile of v3, /device:TPU:0, one launch (start us, length us, event | category | flops | bytes accessed | tf_op | source)
XLA Modules:
  0.0 39.4 jit_solution(12741037088116972324)
XLA Ops:
  0.7 3.2 %shard_map.64 = bf16[1152,128]{1,0:T(8,128)(2,1)} custom-call(s32[1,1]{1,0:T(1,128)S(6)} %copy.7.live_hbm, f32[1,576,512]{2,1,0:T(8,128)} %record_hbm.1, f32[65]{0:T(128)} %band_hbm.1, s32[1,576]{1,0:T(1,128)} %window_hbm.1, s32[1,576]{1,0:T(1,128)} %start_hbm.1), custom_call_target="tpu_custom_call" | custom-call | tf_op jit(solution)/shard_map/pallas_call | solution.py:174
  3.8 7.3 %all-to-all-start = ((bf16[8,144,128]{2,1,0:T(8,128)(2,1)}), bf16[8,144,128]{2,1,0:T(8,128)(2,1)S(1)}, u32[]{:S(2)}, u32[]{:S(2)}) async-start(bf16[8,144,128]{2,1,0:T(8,128)(2,1)} %bitcast.3), calls=%async_computation | async-start | bytes 589824 | tf_op jit(solution)/shard_map/all_to_all | solution.py:518
  11.1 7.6 %shard_map.65.template_hbm.refs_1_.refs_3_ = bf16[144,256,128]{2,1,0:T(8,128)(2,1)} custom-call(bf16[256,144,128]{2,1,0:T(8,128)(2,1)} %template_hbm.1), custom_call_target="tpu_custom_call" | custom-call | flops 9437184 | bytes 18874368 | tf_op jit(solution)/shard_map/pallas_call | solution.py:298
  18.8 2.0 %all-to-all-done = bf16[8,144,128]{2,1,0:T(8,128)(2,1)S(1)} async-done(((bf16[8,144,128]{2,1,0:T(8,128)(2,1)}), bf16[8,144,128]{2,1,0:T(8,128)(2,1)S(1)}, u32[]{:S(2)}, u32[]{:S(2)}) %all-to-all-start) | async-done | bytes 294944 | tf_op jit(solution)/shard_map/all_to_all | solution.py:518
  20.7 1.2 %shard_map.66 = (bf16[36,1152]{1,0:T(8,128)(2,1)S(1)}, bf16[12,256,128]{2,1,0:T(8,128)(2,1)S(1)}) custom-call(bf16[1152,128]{1,0:T(8,128)(2,1)S(1)} %bitcast.2, bf16[144,256,128]{2,1,0:T(8,128)(2,1)} %shard_map.65.template_hbm.refs_1_.refs_3_), custom_call_target="tpu_custom_call" | custom-call | tf_op jit(solution)/shard_map/pallas_call | solution.py:247
  21.9 0.1 collective-permute-start.2
  22.0 1.6 %collective-permute-start.1 = (bf16[36,1152]{1,0:T(8,128)(2,1)S(1)}, bf16[36,1152]{1,0:T(8,128)(2,1)S(1)}, u32[]{:S(2)}, u32[]{:S(2)}) collective-permute-start(bf16[36,1152]{1,0:T(8,128)(2,1)S(1)} %get-tuple-element.11.refs_0_), channel_id=1, source_target_pairs={{0,2},{1,3},{2,0},{3,1},{4,6},{5,7},{6,4},{7,5},{8,10},{9,11},{10,... | collective-permute-start | bytes 248840 | tf_op jit(solution)/shard_map/ppermute | solution.py:523
  23.6 0.3 collective-permute-start
  23.9 4.3 %shard_map.67 = (f32[256,1024]{1,0:T(8,128)S(1)}, f32[9,128]{1,0:T(8,128)S(1)}, f32[256,128]{1,0:T(8,128)S(1)}, bf16[36,256,128]{2,1,0:T(8,128)(2,1)S(1)}) custom-call(bf16[36,1152]{1,0:T(8,128)(2,1)S(1)} %get-tuple-element.11.refs_0_, bf16[144,256,128]{2,1,0:T(8,128)(2,1)} %shard_map.65.template_hbm.refs_1_.refs_3_, ...), custom_call_target="tpu_custom_call" | custom-call | flops 2415919104 | bytes 2359296 | tf_op jit(solution)/shard_map/pallas_call | solution.py:484
  28.2 0.0 collective-permute-done.2.refs_2_
  28.2 0.8 %collective-permute-done.1.refs_1_ = bf16[36,1152]{1,0:T(8,128)(2,1)S(1)} collective-permute-done((bf16[36,1152]{1,0:T(8,128)(2,1)S(1)}, bf16[36,1152]{1,0:T(8,128)(2,1)S(1)}, u32[]{:S(2)}, u32[]{:S(2)}) %collective-permute-start.1) | collective-permute-done | bytes 82976 | tf_op jit(solution)/shard_map/ppermute | solution.py:523
  28.9 0.0 collective-permute-done.refs_0_
  29.0 10.3 %shard_map.68 = f32[256,1024]{1,0:T(8,128)} custom-call(bf16[36,1152]{1,0:T(8,128)(2,1)S(1)} %collective-permute-done.refs_0_, bf16[36,1152]{1,0:T(8,128)(2,1)S(1)} %collective-permute-done.1.refs_1_, bf16[36,1152]{1,0:T(8,128)(2,1)S(1)} %collective-permute-done.2.refs_2_, bf16[144,256,128]{2,1,0:T(8,128)(2,1)} %shard_map.65.template_hbm.refs_1_.refs_3_, ...), custom_call_target="tpu_custom_call" | custom-call | flops 7247757312 | bytes 7077888 | tf_op jit(solution)/shard_map/pallas_call | solution.py:484
Async XLA Ops:
  3.8 16.9 %all-to-all-start = ((bf16[8,144,128]{2,1,0:T(8,128)(2,1)}), bf16[8,144,128]{2,1,0:T(8,128)(2,1)S(1)}, u32[]{:S(2)}, u32[]{:S(2)}) async-start(bf16[8,144,128]{2,1,0:T(8,128)(2,1)} %bitcast.3), calls=%async_computation | async-start | bytes 589824 | tf_op jit(solution)/shard_map/all_to_all | solution.py:518
  21.9 6.2 %collective-permute-start.2 = (bf16[36,1152]{1,0:T(8,128)(2,1)S(1)}, bf16[36,1152]{1,0:T(8,128)(2,1)S(1)}, u32[]{:S(2)}, u32[]{:S(2)}) collective-permute-start(bf16[36,1152]{1,0:T(8,128)(2,1)S(1)} %get-tuple-element.11.refs_0_), channel_id=1, source_target_pairs={{0,3},{1,2},{2,1},{3,0},{4,7},{5,6},{6,5},{7,4},{8,11},{9,10},{10,... | collective-permute-start | bytes 248840 | tf_op jit(solution)/shard_map/ppermute | solution.py:523
  22.0 6.9 %collective-permute-start.1 = (bf16[36,1152]{1,0:T(8,128)(2,1)S(1)}, bf16[36,1152]{1,0:T(8,128)(2,1)S(1)}, u32[]{:S(2)}, u32[]{:S(2)}) collective-permute-start(bf16[36,1152]{1,0:T(8,128)(2,1)S(1)} %get-tuple-element.11.refs_0_), channel_id=1, source_target_pairs={{0,2},{1,3},{2,0},{3,1},{4,6},{5,7},{6,4},{7,5},{8,10},{9,11},{10,... | collective-permute-start | bytes 248840 | tf_op jit(solution)/shard_map/ppermute | solution.py:523
  23.6 5.3 %collective-permute-start = (bf16[36,1152]{1,0:T(8,128)(2,1)S(1)}, bf16[36,1152]{1,0:T(8,128)(2,1)S(1)}, u32[]{:S(2)}, u32[]{:S(2)}) collective-permute-start(bf16[36,1152]{1,0:T(8,128)(2,1)S(1)} %get-tuple-element.11.refs_0_), channel_id=1, source_target_pairs={{0,1},{1,0},{2,3},{3,2},{4,5},{5,4},{6,7},{7,6},{8,9},{9,8},{10,11... | collective-permute-start | bytes 248840 | tf_op jit(solution)/shard_map/ppermute | solution.py:523

commit v4 on v3

--- a/solution.py
+++ b/solution.py
@@ -58,7 +58,7 @@
     band_hbm,
     window_hbm,
     start_hbm,
-    out_ref,
+    out_hbm,
     live_ref,
     record_ref,
     band_ref,
@@ -67,13 +67,16 @@
     taps,
     labels,
     before,
+    out_ref,
     arrivals,
+    departures,
 ):
     entries, rec_len = record_ref.shape[1:]
     span = rec_len // DEC
     capacity = entries // windows
     stride = 2 * capacity
     width = taps.shape[1]
+    halves = [pl.ds(first, entries // 2) for first in (0, entries // 2)]
     copies = [
         pltpu.make_async_copy(source, target, arrivals.at[index])
         for index, (source, target) in enumerate(
@@ -82,7 +85,7 @@
                 (window_hbm, window_ref),
                 (start_hbm, start_ref),
                 (live_hbm, live_ref),
-                (record_hbm, record_ref),
+                *[(record_hbm.at[:, rows], record_ref.at[:, rows]) for rows in halves],
             ]
         )
     ]
@@ -129,14 +132,17 @@
         jnp.sum(jnp.where(ahead, count[windows:] + (first + capacity), 0.0), 0, keepdims=True) - 1.0
     )
 
-    copies[4].wait()
     contract = (((1,), (1,)), ((), ()))
-    record = record_ref[0]
-    record_high = record.astype(BF)
-    record_low = (record - record_high.astype(F32)).astype(BF)
-    upper = lax.dot_general(record_high, filters, contract, preferred_element_type=F32)
-    lower = lax.dot_general(record_low, filters, contract, preferred_element_type=F32)
-    value = upper[:, :LANES] + (upper[:, LANES:] + (lower[:, :LANES] + lower[:, LANES:]))
+    values = []
+    for rows, copy in zip(halves, copies[4:]):
+        copy.wait()
+        record = record_ref[0, rows]
+        record_high = record.astype(BF)
+        record_low = (record - record_high.astype(F32)).astype(BF)
+        upper = lax.dot_general(record_high, filters, contract, preferred_element_type=F32)
+        lower = lax.dot_general(record_low, filters, contract, preferred_element_type=F32)
+        values.append(upper[:, :LANES] + (upper[:, LANES:] + (lower[:, :LANES] + lower[:, LANES:])))
+    value = jnp.concatenate(values, 0)
     high = value.astype(BF).astype(F32)
     rest = value - high
     middle = rest.astype(BF).astype(F32)
@@ -152,6 +158,7 @@
     plain = capacity % 8 == 0
     part = stride if plain else total // 4
     row = lax.broadcasted_iota(jnp.int32, (part, entries), 0).astype(F32)
+    sends = []
     for index in range(total // part):
         here, there = place - float(index * part), place_ahead - float(index * part)
         if plain:
@@ -167,6 +174,11 @@
         out_ref[index * part : (index + 1) * part, :] = jnp.dot(
             chosen.astype(BF), payload, preferred_element_type=F32
         ).astype(BF)
+        span_of = pl.ds(index * part, part)
+        sends.append(pltpu.make_async_copy(out_ref.at[span_of], out_hbm.at[span_of], departures.at[index]))
+        sends[-1].start()
+    for copy in sends:
+        copy.wait()
 
 
 def pack(records, band_filter, windows_of, starts, live, slots, windows):
@@ -175,7 +187,7 @@
         functools.partial(pack_kernel, slots, windows),
         out_shape=jax.ShapeDtypeStruct((2 * entries, LANES), BF),
         in_specs=[whole(pltpu.HBM)] * 5,
-        out_specs=whole(),
+        out_specs=whole(pltpu.HBM),
         scratch_shapes=[
             pltpu.SMEM(live.shape, live.dtype),
             pltpu.VMEM(records.shape, F32),
@@ -185,7 +197,9 @@
             pltpu.VMEM((8, rec_len + LANES), F32),
             pltpu.VMEM((LANES, pl.cdiv(entries, LANES) * LANES), F32),
             pltpu.VMEM((entries, entries), BF),
-            pltpu.SemaphoreType.DMA((5,)),
+            pltpu.VMEM((2 * entries, LANES), BF),
+            pltpu.SemaphoreType.DMA((6,)),
+            pltpu.SemaphoreType.DMA((max(windows, 4),)),
         ],
         compiler_params=pltpu.CompilerParams(vmem_limit_bytes=60 * MIB),
     )(live, records, band_filter, windows_of, starts)

time: 39.7 us -> 39.7 us (level)
  no operation moved by 1% of the time
where the time goes in v4:
time: 39.7 us; the launch traced here: 39.4 us
  Pallas kernels  26.6 us (67%)
  starting transfers between devices  9.19 us (23%)
  waiting for transfers between devices  2.71 us (7%)
  between operations  0.86 us (2%)
    pallas_call x2, Pallas kernels, correlate(): pl.pallas_call(functools.partial(correlate_kernel, steps, bool(begun)), o...  14.6 us
    pallas_call x1, Pallas kernels, regroup(): pl.pallas_call(regroup_kernel, in_specs=[whole(pltpu.HBM)], out_specs=who...  7.65 us
    all_to_all x1, starting transfers between devices, shards(): lax.all_to_all(outgoing, 'tm', split_axis=0, concat_axis=0, tiled=True)  7.28 us
    pallas_call x1, Pallas kernels, pack(): pl.pallas_call(functools.partial(pack_kernel, slots, windows), out_shape=...  3.16 us
    all_to_all x1, waiting for transfers between devices, shards(): lax.all_to_all(outgoing, 'tm', split_axis=0, concat_axis=0, tiled=True)  1.95 us
    ppermute x3, starting transfers between devices, shards(): lax.ppermute(own, 'tmpl', [(source, source ^ step) for source in range(qu...  1.92 us
    pallas_call x1, Pallas kernels, arrange(): pl.pallas_call(functools.partial(arrange_kernel, slots, stride), out_shap...  1.22 us
  transfers between devices with their start and end apart: 4, of which 2 were waited for; matrix products, arithmetic and copies ran while one was open for 0% of the time, Pallas kernels for 30%

profile of v4, /device:TPU:0, one launch (start us, length us, event | category | flops | bytes accessed | tf_op | source)
XLA Modules:
  0.0 39.4 jit_solution(1901244283356603845)
XLA Ops:
  0.7 3.2 %shard_map.64 = bf16[1152,128]{1,0:T(8,128)(2,1)} custom-call(s32[1,1]{1,0:T(1,128)S(6)} %copy.7.live_hbm, f32[1,576,512]{2,1,0:T(8,128)} %record_hbm.1, f32[65]{0:T(128)} %band_hbm.1, s32[1,576]{1,0:T(1,128)} %window_hbm.1, s32[1,576]{1,0:T(1,128)} %start_hbm.1), custom_call_target="tpu_custom_call" | custom-call | tf_op jit(solution)/shard_map/pallas_call | solution.py:186
  3.8 7.3 %all-to-all-start = ((bf16[8,144,128]{2,1,0:T(8,128)(2,1)}), bf16[8,144,128]{2,1,0:T(8,128)(2,1)S(1)}, u32[]{:S(2)}, u32[]{:S(2)}) async-start(bf16[8,144,128]{2,1,0:T(8,128)(2,1)} %bitcast.3), calls=%async_computation | async-start | bytes 589824 | tf_op jit(solution)/shard_map/all_to_all | solution.py:532
  11.1 7.6 %shard_map.65.template_hbm.refs_1_.refs_3_ = bf16[144,256,128]{2,1,0:T(8,128)(2,1)} custom-call(bf16[256,144,128]{2,1,0:T(8,128)(2,1)} %template_hbm.1), custom_call_target="tpu_custom_call" | custom-call | flops 9437184 | bytes 18874368 | tf_op jit(solution)/shard_map/pallas_call | solution.py:312
  18.8 2.0 %all-to-all-done = bf16[8,144,128]{2,1,0:T(8,128)(2,1)S(1)} async-done(((bf16[8,144,128]{2,1,0:T(8,128)(2,1)}), bf16[8,144,128]{2,1,0:T(8,128)(2,1)S(1)}, u32[]{:S(2)}, u32[]{:S(2)}) %all-to-all-start) | async-done | bytes 294944 | tf_op jit(solution)/shard_map/all_to_all | solution.py:532
  20.7 1.2 %shard_map.66 = (bf16[36,1152]{1,0:T(8,128)(2,1)S(1)}, bf16[12,256,128]{2,1,0:T(8,128)(2,1)S(1)}) custom-call(bf16[1152,128]{1,0:T(8,128)(2,1)S(1)} %bitcast.2, bf16[144,256,128]{2,1,0:T(8,128)(2,1)} %shard_map.65.template_hbm.refs_1_.refs_3_), custom_call_target="tpu_custom_call" | custom-call | tf_op jit(solution)/shard_map/pallas_call | solution.py:261
  21.9 0.1 collective-permute-start.2
  22.0 1.6 %collective-permute-start.1 = (bf16[36,1152]{1,0:T(8,128)(2,1)S(1)}, bf16[36,1152]{1,0:T(8,128)(2,1)S(1)}, u32[]{:S(2)}, u32[]{:S(2)}) collective-permute-start(bf16[36,1152]{1,0:T(8,128)(2,1)S(1)} %get-tuple-element.11.refs_0_), channel_id=1, source_target_pairs={{0,2},{1,3},{2,0},{3,1},{4,6},{5,7},{6,4},{7,5},{8,10},{9,11},{10,... | collective-permute-start | bytes 248840 | tf_op jit(solution)/shard_map/ppermute | solution.py:537
  23.6 0.3 collective-permute-start
  23.9 4.3 %shard_map.67 = (f32[256,1024]{1,0:T(8,128)S(1)}, f32[9,128]{1,0:T(8,128)S(1)}, f32[256,128]{1,0:T(8,128)S(1)}, bf16[36,256,128]{2,1,0:T(8,128)(2,1)S(1)}) custom-call(bf16[36,1152]{1,0:T(8,128)(2,1)S(1)} %get-tuple-element.11.refs_0_, bf16[144,256,128]{2,1,0:T(8,128)(2,1)} %shard_map.65.template_hbm.refs_1_.refs_3_, ...), custom_call_target="tpu_custom_call" | custom-call | flops 2415919104 | bytes 2359296 | tf_op jit(solution)/shard_map/pallas_call | solution.py:498
  28.2 0.0 collective-permute-done.2.refs_2_
  28.2 0.8 %collective-permute-done.1.refs_1_ = bf16[36,1152]{1,0:T(8,128)(2,1)S(1)} collective-permute-done((bf16[36,1152]{1,0:T(8,128)(2,1)S(1)}, bf16[36,1152]{1,0:T(8,128)(2,1)S(1)}, u32[]{:S(2)}, u32[]{:S(2)}) %collective-permute-start.1) | collective-permute-done | bytes 82976 | tf_op jit(solution)/shard_map/ppermute | solution.py:537
  28.9 0.0 collective-permute-done.refs_0_
  28.9 10.3 %shard_map.68 = f32[256,1024]{1,0:T(8,128)} custom-call(bf16[36,1152]{1,0:T(8,128)(2,1)S(1)} %collective-permute-done.refs_0_, bf16[36,1152]{1,0:T(8,128)(2,1)S(1)} %collective-permute-done.1.refs_1_, bf16[36,1152]{1,0:T(8,128)(2,1)S(1)} %collective-permute-done.2.refs_2_, bf16[144,256,128]{2,1,0:T(8,128)(2,1)} %shard_map.65.template_hbm.refs_1_.refs_3_, ...), custom_call_target="tpu_custom_call" | custom-call | flops 7247757312 | bytes 7077888 | tf_op jit(solution)/shard_map/pallas_call | solution.py:498
Async XLA Ops:
  3.8 16.9 %all-to-all-start = ((bf16[8,144,128]{2,1,0:T(8,128)(2,1)}), bf16[8,144,128]{2,1,0:T(8,128)(2,1)S(1)}, u32[]{:S(2)}, u32[]{:S(2)}) async-start(bf16[8,144,128]{2,1,0:T(8,128)(2,1)} %bitcast.3), calls=%async_computation | async-start | bytes 589824 | tf_op jit(solution)/shard_map/all_to_all | solution.py:532
  21.9 6.2 %collective-permute-start.2 = (bf16[36,1152]{1,0:T(8,128)(2,1)S(1)}, bf16[36,1152]{1,0:T(8,128)(2,1)S(1)}, u32[]{:S(2)}, u32[]{:S(2)}) collective-permute-start(bf16[36,1152]{1,0:T(8,128)(2,1)S(1)} %get-tuple-element.11.refs_0_), channel_id=1, source_target_pairs={{0,3},{1,2},{2,1},{3,0},{4,7},{5,6},{6,5},{7,4},{8,11},{9,10},{10,... | collective-permute-start | bytes 248840 | tf_op jit(solution)/shard_map/ppermute | solution.py:537
  22.0 6.9 %collective-permute-start.1 = (bf16[36,1152]{1,0:T(8,128)(2,1)S(1)}, bf16[36,1152]{1,0:T(8,128)(2,1)S(1)}, u32[]{:S(2)}, u32[]{:S(2)}) collective-permute-start(bf16[36,1152]{1,0:T(8,128)(2,1)S(1)} %get-tuple-element.11.refs_0_), channel_id=1, source_target_pairs={{0,2},{1,3},{2,0},{3,1},{4,6},{5,7},{6,4},{7,5},{8,10},{9,11},{10,... | collective-permute-start | bytes 248840 | tf_op jit(solution)/shard_map/ppermute | solution.py:537
  23.6 5.3 %collective-permute-start = (bf16[36,1152]{1,0:T(8,128)(2,1)S(1)}, bf16[36,1152]{1,0:T(8,128)(2,1)S(1)}, u32[]{:S(2)}, u32[]{:S(2)}) collective-permute-start(bf16[36,1152]{1,0:T(8,128)(2,1)S(1)} %get-tuple-element.11.refs_0_), channel_id=1, source_target_pairs={{0,1},{1,0},{2,3},{3,2},{4,5},{5,4},{6,7},{7,6},{8,9},{9,8},{10,11... | collective-permute-start | bytes 248840 | tf_op jit(solution)/shard_map/ppermute | solution.py:537

commit v5 on v3

--- a/solution.py
+++ b/solution.py
@@ -248,7 +248,7 @@
         functools.partial(arrange_kernel, slots, stride),
         out_shape=[
             jax.ShapeDtypeStruct((channels, (slots // 2 + 1) * LANES), BF),
-            jax.ShapeDtypeStruct((channels // 3, *templates.shape[1:]), BF),
+            jax.ShapeDtypeStruct((channels // 6, *templates.shape[1:]), BF),
         ],
         in_specs=[whole(), whole(pltpu.HBM)],
         out_specs=[whole(), whole()],

time: 39.7 us -> 39.7 us (level)
  Pallas kernels: 26.7 us -> 26.2 us
  waiting for transfers between devices: 2.71 us -> 3.15 us
    pallas_call x2, Pallas kernels: 14.6 us -> 14.2 us  [correlate(): pl.pallas_call(functools.partial(correlate_kernel, steps, bool(begun)), o...]
    ppermute x3, waiting for transfers between devices: 0.76 us -> 1.19 us  [shards(): lax.ppermute(own, 'tmpl', [(source, source ^ step) for source in range(qu...]
  transfers between devices with their start and end apart: 4 -> 4, of which waited for: 2 -> 2; matrix products, arithmetic and copies ran while one was open for 0% -> 0% of each run, Pallas kernels for 30% -> 29%
where the time goes in v5:
time: 39.7 us; the launch traced here: 39.4 us
  Pallas kernels  26.2 us (66%)
  starting transfers between devices  9.19 us (23%)
  waiting for transfers between devices  3.15 us (8%)
  between operations  0.86 us (2%)
    pallas_call x2, Pallas kernels, correlate(): pl.pallas_call(functools.partial(correlate_kernel, steps, bool(begun)), o...  14.2 us
    pallas_call x1, Pallas kernels, regroup(): pl.pallas_call(regroup_kernel, in_specs=[whole(pltpu.HBM)], out_specs=who...  7.65 us
    all_to_all x1, starting transfers between devices, shards(): lax.all_to_all(outgoing, 'tm', split_axis=0, concat_axis=0, tiled=True)  7.27 us
    pallas_call x1, Pallas kernels, pack(): pl.pallas_call(functools.partial(pack_kernel, slots, windows), out_shape=...  3.18 us
    all_to_all x1, waiting for transfers between devices, shards(): lax.all_to_all(outgoing, 'tm', split_axis=0, concat_axis=0, tiled=True)  1.96 us
    ppermute x3, starting transfers between devices, shards(): lax.ppermute(own, 'tmpl', [(source, source ^ step) for source in range(qu...  1.92 us
    pallas_call x1, Pallas kernels, arrange(): pl.pallas_call(functools.partial(arrange_kernel, slots, stride), out_shap...  1.22 us
    ppermute x3, waiting for transfers between devices, shards(): lax.ppermute(own, 'tmpl', [(source, source ^ step) for source in range(qu...  1.19 us
  transfers between devices with their start and end apart: 4, of which 2 were waited for; matrix products, arithmetic and copies ran while one was open for 0% of the time, Pallas kernels for 29%

profile of v5, /device:TPU:0, one launch (start us, length us, event | category | flops | bytes accessed | tf_op | source)
XLA Modules:
  0.0 39.4 jit_solution(7314300726306388797)
XLA Ops:
  0.7 3.2 %shard_map.64 = bf16[1152,128]{1,0:T(8,128)(2,1)} custom-call(s32[1,1]{1,0:T(1,128)S(6)} %copy.7.live_hbm, f32[1,576,512]{2,1,0:T(8,128)} %record_hbm.1, f32[65]{0:T(128)} %band_hbm.1, s32[1,576]{1,0:T(1,128)} %window_hbm.1, s32[1,576]{1,0:T(1,128)} %start_hbm.1), custom_call_target="tpu_custom_call" | custom-call | tf_op jit(solution)/shard_map/pallas_call | solution.py:174
  3.8 7.3 %all-to-all-start = ((bf16[8,144,128]{2,1,0:T(8,128)(2,1)}), bf16[8,144,128]{2,1,0:T(8,128)(2,1)S(1)}, u32[]{:S(2)}, u32[]{:S(2)}) async-start(bf16[8,144,128]{2,1,0:T(8,128)(2,1)} %bitcast.3), calls=%async_computation | async-start | bytes 589824 | tf_op jit(solution)/shard_map/all_to_all | solution.py:518
  11.1 7.6 %shard_map.65.template_hbm.refs_1_.refs_3_ = bf16[144,256,128]{2,1,0:T(8,128)(2,1)} custom-call(bf16[256,144,128]{2,1,0:T(8,128)(2,1)} %template_hbm.1), custom_call_target="tpu_custom_call" | custom-call | flops 9437184 | bytes 18874368 | tf_op jit(solution)/shard_map/pallas_call | solution.py:298
  18.8 2.0 %all-to-all-done = bf16[8,144,128]{2,1,0:T(8,128)(2,1)S(1)} async-done(((bf16[8,144,128]{2,1,0:T(8,128)(2,1)}), bf16[8,144,128]{2,1,0:T(8,128)(2,1)S(1)}, u32[]{:S(2)}, u32[]{:S(2)}) %all-to-all-start) | async-done | bytes 294944 | tf_op jit(solution)/shard_map/all_to_all | solution.py:518
  20.7 1.2 %shard_map.66 = (bf16[36,1152]{1,0:T(8,128)(2,1)S(1)}, bf16[6,256,128]{2,1,0:T(8,128)(2,1)S(1)}) custom-call(bf16[1152,128]{1,0:T(8,128)(2,1)S(1)} %bitcast.2, bf16[144,256,128]{2,1,0:T(8,128)(2,1)} %shard_map.65.template_hbm.refs_1_.refs_3_), custom_call_target="tpu_custom_call" | custom-call | tf_op jit(solution)/shard_map/pallas_call | solution.py:247
  21.9 0.1 collective-permute-start.2
  22.0 1.6 %collective-permute-start.1 = (bf16[36,1152]{1,0:T(8,128)(2,1)S(1)}, bf16[36,1152]{1,0:T(8,128)(2,1)S(1)}, u32[]{:S(2)}, u32[]{:S(2)}) collective-permute-start(bf16[36,1152]{1,0:T(8,128)(2,1)S(1)} %get-tuple-element.11.refs_0_), channel_id=1, source_target_pairs={{0,2},{1,3},{2,0},{3,1},{4,6},{5,7},{6,4},{7,5},{8,10},{9,11},{10,... | collective-permute-start | bytes 248840 | tf_op jit(solution)/shard_map/ppermute | solution.py:523
  23.6 0.3 collective-permute-start
  23.9 3.9 %shard_map.67 = (f32[256,1024]{1,0:T(8,128)S(1)}, f32[9,128]{1,0:T(8,128)S(1)}, f32[256,128]{1,0:T(8,128)S(1)}, bf16[36,256,128]{2,1,0:T(8,128)(2,1)S(1)}) custom-call(bf16[36,1152]{1,0:T(8,128)(2,1)S(1)} %get-tuple-element.11.refs_0_, bf16[144,256,128]{2,1,0:T(8,128)(2,1)} %shard_map.65.template_hbm.refs_1_.refs_3_, ...), custom_call_target="tpu_custom_call" | custom-call | flops 2415919104 | bytes 2359296 | tf_op jit(solution)/shard_map/pallas_call | solution.py:484
  27.7 0.0 collective-permute-done.2.refs_2_
  27.8 1.2 %collective-permute-done.1.refs_1_ = bf16[36,1152]{1,0:T(8,128)(2,1)S(1)} collective-permute-done((bf16[36,1152]{1,0:T(8,128)(2,1)S(1)}, bf16[36,1152]{1,0:T(8,128)(2,1)S(1)}, u32[]{:S(2)}, u32[]{:S(2)}) %collective-permute-start.1) | collective-permute-done | bytes 82976 | tf_op jit(solution)/shard_map/ppermute | solution.py:523
  28.9 0.0 collective-permute-done.refs_0_
  29.0 10.3 %shard_map.68 = f32[256,1024]{1,0:T(8,128)} custom-call(bf16[36,1152]{1,0:T(8,128)(2,1)S(1)} %collective-permute-done.refs_0_, bf16[36,1152]{1,0:T(8,128)(2,1)S(1)} %collective-permute-done.1.refs_1_, bf16[36,1152]{1,0:T(8,128)(2,1)S(1)} %collective-permute-done.2.refs_2_, bf16[144,256,128]{2,1,0:T(8,128)(2,1)} %shard_map.65.template_hbm.refs_1_.refs_3_, ...), custom_call_target="tpu_custom_call" | custom-call | flops 7247757312 | bytes 7077888 | tf_op jit(solution)/shard_map/pallas_call | solution.py:484
Async XLA Ops:
  3.8 16.9 %all-to-all-start = ((bf16[8,144,128]{2,1,0:T(8,128)(2,1)}), bf16[8,144,128]{2,1,0:T(8,128)(2,1)S(1)}, u32[]{:S(2)}, u32[]{:S(2)}) async-start(bf16[8,144,128]{2,1,0:T(8,128)(2,1)} %bitcast.3), calls=%async_computation | async-start | bytes 589824 | tf_op jit(solution)/shard_map/all_to_all | solution.py:518
  21.9 5.8 %collective-permute-start.2 = (bf16[36,1152]{1,0:T(8,128)(2,1)S(1)}, bf16[36,1152]{1,0:T(8,128)(2,1)S(1)}, u32[]{:S(2)}, u32[]{:S(2)}) collective-permute-start(bf16[36,1152]{1,0:T(8,128)(2,1)S(1)} %get-tuple-element.11.refs_0_), channel_id=1, source_target_pairs={{0,3},{1,2},{2,1},{3,0},{4,7},{5,6},{6,5},{7,4},{8,11},{9,10},{10,... | collective-permute-start | bytes 248840 | tf_op jit(solution)/shard_map/ppermute | solution.py:523
  22.0 6.9 %collective-permute-start.1 = (bf16[36,1152]{1,0:T(8,128)(2,1)S(1)}, bf16[36,1152]{1,0:T(8,128)(2,1)S(1)}, u32[]{:S(2)}, u32[]{:S(2)}) collective-permute-start(bf16[36,1152]{1,0:T(8,128)(2,1)S(1)} %get-tuple-element.11.refs_0_), channel_id=1, source_target_pairs={{0,2},{1,3},{2,0},{3,1},{4,6},{5,7},{6,4},{7,5},{8,10},{9,11},{10,... | collective-permute-start | bytes 248840 | tf_op jit(solution)/shard_map/ppermute | solution.py:523
  23.6 5.3 %collective-permute-start = (bf16[36,1152]{1,0:T(8,128)(2,1)S(1)}, bf16[36,1152]{1,0:T(8,128)(2,1)S(1)}, u32[]{:S(2)}, u32[]{:S(2)}) collective-permute-start(bf16[36,1152]{1,0:T(8,128)(2,1)S(1)} %get-tuple-element.11.refs_0_), channel_id=1, source_target_pairs={{0,1},{1,0},{2,3},{3,2},{4,5},{5,4},{6,7},{7,6},{8,9},{9,8},{10,11... | collective-permute-start | bytes 248840 | tf_op jit(solution)/shard_map/ppermute | solution.py:523
